TPU v7x, 512 devices: a whole 4x8x8 slice. The times are simulated.
512 devices in a mesh: layer: 4 (over x), seq: 16 (over y, core), tile: 8 (over z).
Axes of the slice: x: 4, y: 8, z: 8, core: 2. Of those that a mesh axis runs over, the one named last changes fastest.
Arguments:
- activations: bfloat16 [16, 3072, 4096], P('layer', 'seq', 'tile'), parts along dimension 0, may hold values from -6 to 6
- out_grads: bfloat16 [16, 3072, 14336], P('layer', 'seq', 'tile'), parts along dimension 0, may hold values from -6 to 6
- proj_in: bfloat16 [16384, 128], P(('layer', 'tile')), parts along dimension 0, may hold values from -0.09375 to 0.09375
- proj_out: bfloat16 [57344, 256], P(('layer', 'tile')), parts along dimension 0, may hold values from -0.046875 to 0.046875
- seq_lengths: int32 [4], replicated, may hold values from 1 to 3072, 7680 in all
- tile_map: int32 [128, 2], replicated, may hold values from 0 to 127, as said below
- prior_cov: float32 [512, 256, 256], P(('layer', 'seq', 'tile')), parts along dimension 0, may hold values from -6 to 6
Outputs:
- covariance: float32 [512, 256, 256], P(('layer', 'seq', 'tile')), parts along dimension 0
There are 4 independent parts, one for each index of `layer`. A program takes and returns all parts, laid end to end along the dimension named above; an argument that names none is the same for every part. Nothing has to cross between parts.
Inputs may be any that keep to these rules, and one draw needn't show every extreme that they name: `tile_map`: each row holds two feature block numbers, the first not above the second; rows may repeat.
All inputs are finite; a program needn't handle non-finite values.
Results may differ from a plain program's by a relative error of at most 0.0003.
Values sent between devices are 32-bit elements; how exact they have to be, the bound alone decides.
No kernel may reach another device: no remote copies, remote signals or barrier semaphores. Data moves between devices by JAX's collectives and lax.ppermute only.
A program may use at most 192 MiB of HBM per device.

v0:
```python
import jax
import jax.numpy as jnp
from jax import lax
from jax.sharding import PartitionSpec as P


def project_tokens(act_rows, grad_rows, proj_in, proj_out):
    left_side = jnp.einsum("slc,ck->lsk", act_rows, proj_in, preferred_element_type=jnp.float32)
    right_side = jnp.einsum("slc,ck->lsk", grad_rows, proj_out, preferred_element_type=jnp.float32)
    return jnp.concatenate([left_side, right_side], axis=2)


def body(activations, out_grads, proj_in, proj_out, seq_lengths, tile_map, prior_cov):
    tiles_here = prior_cov.shape[0]
    block_size = prior_cov.shape[1]
    seq_count = activations.shape[0]
    tok_len = activations.shape[1]
    width_in = proj_in.shape[1]
    width_out = proj_out.shape[1]
    tile_count = lax.axis_size("tile")
    tok_rows = tok_len // tile_count
    whole_term = project_tokens(activations, out_grads, proj_in, proj_out)
    totals = lax.psum(whole_term, "tile")
    summed = lax.dynamic_slice_in_dim(totals, lax.axis_index("tile") * tok_rows, tok_rows, 0)
    positions = (
        lax.axis_index("seq") * tok_len
        + lax.axis_index("tile") * tok_rows
        + jnp.arange(tok_rows, dtype=jnp.int32)
    )
    token_mask = (positions[:, None] < seq_lengths[None, :]).astype(jnp.float32)
    token_weight = token_mask * lax.rsqrt(seq_lengths.astype(jnp.float32))[None, :]
    left_part = summed[:, :, :width_in]
    right_part = summed[:, :, width_in:] * token_weight[:, :, None]
    partial_value = jnp.einsum(
        "lsj,lsi->sji", right_part, left_part, precision=lax.Precision.HIGHEST
    )
    partial_value = partial_value.reshape(seq_count, width_out * width_in)
    offsets = jnp.arange(block_size, dtype=jnp.int32)
    features = lax.psum_scatter(partial_value, ("seq", "tile"), scatter_dimension=1, tiled=True)
    owner_index = lax.axis_index(("seq", "tile"))
    own_pairs = lax.dynamic_slice_in_dim(tile_map, owner_index * tiles_here, tiles_here, 0)
    shard_piece = lax.all_gather(features, ("seq", "tile"), axis=1, tiled=True)
    piece_width = shard_piece.shape[1]
    columns = own_pairs[:, :, None] * block_size + offsets
    inside = (columns >= 0) & (columns < piece_width)
    picked = jnp.take(shard_piece, jnp.clip(columns, 0, piece_width - 1), axis=1)
    picked = jnp.where(inside[None], picked, 0.0)
    chosen = jnp.transpose(picked, (1, 2, 0, 3))
    product = jnp.einsum(
        "kse,ksf->kef", chosen[:, 0], chosen[:, 1], precision=lax.Precision.HIGHEST
    )
    return prior_cov + product


def solution(mesh):
    return jax.shard_map(
        body,
        mesh=mesh,
        in_specs=(
            P("layer", "seq", "tile"),
            P("layer", "seq", "tile"),
            P(("layer", "tile"), None),
            P(("layer", "tile"), None),
            P(),
            P(),
            P(("layer", "seq", "tile"), None, None),
        ),
        out_specs=P(("layer", "seq", "tile"), None, None),
        check_vma=False,
    )
```

profile of v0, /device:TPU:6, one launch (start us, length us, event | category | flops | bytes accessed | tf_op | source)
XLA Modules:
  0.0 483.9 jit_solution(7159621079205856472)
XLA Ops:
  6.5 0.0 copy-start
  6.5 0.0 all-reduce.2.cloned.1.call-start
  6.5 1.8 copy-done
  8.3 2.1 convolution_bitcast_fusion
  10.4 0.0 copy-done.1
  10.4 0.4 convolution_bitcast_fusion.1
  10.8 1.1 pad_maximum_fusion
  11.9 0.0 all-reduce.2.cloned.1.call-update
  12.0 0.0 reduce-scatter.2.cloned.1.call-start
  12.0 0.6 copy-done.5
  12.6 0.1 compare_select_fusion.2
  12.7 86.7 %all-reduce.2.cloned.1.call-done = f32[192,4,384]{2,0,1:T(8,128)} async-done(((f32[192,4,384]{2,0,1:T(8,128)}), f32[192,4,384]{2,0,1:T(8,128)}) %all-reduce.2.cloned.1.call-update) | async-done | bytes 1179664 | tf_op jit(solution)/shard_map/psum | solution.py:23
  99.3 2.0 fusion.3
  101.3 8.7 %copy.10 = f32[4,256,128]{0,2,1:T(8,128)} copy(f32[4,256,128]{2,1,0:T(8,128)S(1)} %fusion.3) | data formatting | bytes 1048576 | tf_op jit(solution)/shard_map/reshape | solution.py:37
  110.0 0.0 reduce-scatter.2.cloned.1.call-update
  110.1 0.6 copy-done.4
  110.7 0.2 multiply_reduce_fusion
  110.9 0.1 fusion.6
  111.0 0.1 compare_and_fusion.1
  111.1 221.1 %reduce-scatter.2.cloned.1.call-done = f32[4,256]{0,1:T(8,128)} async-done(((f32[4,32768]{0,1:T(8,128)}), f32[4,256]{0,1:T(8,128)}) %reduce-scatter.2.cloned.1.call-update) | async-done | bytes 4112 | tf_op jit(solution)/shard_map/reduce_scatter | solution.py:39
  332.2 136.7 %all_gather.3 = f32[4,32768]{0,1:T(8,128)} all-gather(f32[4,256]{0,1:T(8,128)} %reduce-scatter.2.cloned.1.call-done), channel_id=1, replica_groups=mesh['layer'=4,'seq'=16,'tile'=8] {'seq','tile'}, dimensions={1}, use_global_device_ids=true | all-gather | bytes 528384 | tf_op jit(solution)/shard_map/all_gather | solution.py:42
  469.0 6.8 %gather_fusion = f32[512,4]{1,0:T(8,128)S(1)} fusion(f32[4,32768]{0,1:T(8,128)} %all_gather.3, s32[1024]{0:T(1024)S(1)} %pad_clamp_fusion), kind=kCustom, calls=%fused_computation | custom fusion | bytes 18432 | tf_op jit(solution)/shard_map/jit(_take)/gather | solution.py:46
  475.8 0.2 select_bitcast_fusion
  476.0 1.1 fusion
  (11 shorter events, 0.0 us)
Async XLA Ops:
  6.5 1.8 copy-start
  6.5 3.9 copy-start.1
  6.5 92.8 %all-reduce.2.cloned.1.call-start = ((), (), s32[]{:S(2)}) async-start(), calls=%async_computation.1 | async-start | bytes 2359296 | tf_op jit(solution)/shard_map/psum | solution.py:23
  8.3 2.1 copy-start.3
  11.9 0.7 copy-start.5
  12.0 320.3 %reduce-scatter.2.cloned.1.call-start = ((), (), s32[]{:S(2)}) async-start(), calls=%async_computation.2 | async-start | bytes 16908288 | tf_op jit(solution)/shard_map/reduce_scatter | solution.py:39
  110.0 0.7 copy-start.4
  111.1 364.9 %copy-start.2 = (f32[1,256,256]{2,1,0:T(8,128)S(1)}, f32[1,256,256]{2,1,0:T(8,128)}, u32[]{:S(2)}) copy-start(f32[1,256,256]{2,1,0:T(8,128)} %param.13) | copy-start | bytes 786436
Sparse Core Ops, SparseCore 0:
  12.1 87.2 all-reduce.1
  110.2 221.9 reduce-scatter.1
where the time goes:
time: 484 us
  waiting for transfers between devices  308 us (64%)
  blocking collectives  137 us (28%)
  local copies, waits for them, and re-layouts  18.5 us (4%)
  between operations  13.5 us (3%)
  matrix products  5.56 us (1%)
    reduce_scatter x1, waiting for transfers between devices, body(): lax.psum_scatter(partial_value, ('seq', 'tile'), scatter_dimension=1, til...  221 us
    all_gather x1, blocking collectives, body(): shard_piece = lax.all_gather(features, ('seq', 'tile'), axis=1, tiled=True)  137 us
    psum x1, waiting for transfers between devices, body(): totals = lax.psum(whole_term, 'tile')  86.7 us
  transfers between devices with their start and end apart: 2, of which 2 were waited for; matrix products, arithmetic and copies ran while one was open for 0% of the time, Pallas kernels for 0%

commit v1 on v0

v1 whole, which is shorter than its diff:
```python
import functools

import jax
import jax.numpy as jnp
from jax import lax
from jax.experimental import pallas as pl
from jax.experimental.pallas import tpu as pltpu
from jax.sharding import Mesh
from jax.sharding import PartitionSpec as P

HIGHEST = lax.Precision.HIGHEST
VMEM_LIMIT = 32 * 1024 * 1024


def project_kernel(act_ref, grad_ref, in_ref, out_ref, o_ref):
    width_in = in_ref.shape[1]
    pieces, _, rows, width = o_ref.shape
    left = jnp.dot(act_ref[0], in_ref[...], preferred_element_type=jnp.float32)
    right = jnp.dot(grad_ref[0], out_ref[...], preferred_element_type=jnp.float32)
    o_ref[:, 0, :, :width_in] = left.reshape(pieces, rows, width_in)
    o_ref[:, 0, :, width_in:] = right.reshape(pieces, rows, width - width_in)


def project(activations, out_grads, proj_in, proj_out, pieces):
    seqs, tok, dim = activations.shape
    hidden = out_grads.shape[2]
    width_in, width_out = proj_in.shape[1], proj_out.shape[1]
    rows, width = tok // pieces, width_in + width_out
    return pl.pallas_call(
        project_kernel,
        grid=(seqs,),
        out_shape=jax.ShapeDtypeStruct((pieces, seqs, rows, width), jnp.float32),
        in_specs=[
            pl.BlockSpec((1, tok, dim), lambda s: (s, 0, 0)),
            pl.BlockSpec((1, tok, hidden), lambda s: (s, 0, 0)),
            pl.BlockSpec((dim, width_in), lambda s: (0, 0)),
            pl.BlockSpec((hidden, width_out), lambda s: (0, 0)),
        ],
        out_specs=pl.BlockSpec((pieces, 1, rows, width), lambda s: (0, s, 0, 0)),
        compiler_params=pltpu.CompilerParams(vmem_limit_bytes=VMEM_LIMIT),
        cost_estimate=pl.CostEstimate(
            flops=2 * seqs * tok * (dim * width_in + hidden * width_out),
            bytes_accessed=2 * seqs * tok * (dim + hidden) + 4 * seqs * tok * width,
            transcendentals=0,
        ),
    )(activations, out_grads, proj_in, proj_out)


def expand_kernel(map_ref, core_ref, own_ref, other_ref, o_ref, grads_ref):
    seqs = own_ref.shape[0]
    width_in = o_ref.shape[1]
    width_out = own_ref.shape[2] - width_in
    for s in range(seqs):
        tokens = jnp.concatenate([own_ref[s], other_ref[s]], axis=0)
        left, right = tokens[:, :width_in], tokens[:, width_in:]
        grads_ref[pl.ds(s, width_out, stride=seqs), :] = lax.dot_general(
            right, left, (((0,), (0,)), ((), ())), precision=HIGHEST, preferred_element_type=jnp.float32
        )
    core = core_ref[0]
    owners = o_ref.shape[0] // 16
    for n in range(owners):
        k = (2 * (n // 8) + core) * 8 + n % 8
        for side in range(2):
            block = map_ref[side, k]
            o_ref[16 * n + 8 * side:16 * n + 8 * side + 8, :] = grads_ref[
                pl.ds(pl.multiple_of(block * 8, 8), 8), :
            ]


def expand(tile_map, core, own, other, owners, width_in):
    seqs, rows, width = own.shape
    width_out = width - width_in
    return pl.pallas_call(
        expand_kernel,
        out_shape=jax.ShapeDtypeStruct((owners * 16, width_in), jnp.float32),
        in_specs=[
            pl.BlockSpec(memory_space=pltpu.SMEM),
            pl.BlockSpec(memory_space=pltpu.SMEM),
            pl.BlockSpec(memory_space=pltpu.VMEM),
            pl.BlockSpec(memory_space=pltpu.VMEM),
        ],
        out_specs=pl.BlockSpec(memory_space=pltpu.VMEM),
        scratch_shapes=[pltpu.VMEM((seqs * width_out, width_in), jnp.float32)],
        compiler_params=pltpu.CompilerParams(vmem_limit_bytes=VMEM_LIMIT),
        cost_estimate=pl.CostEstimate(
            flops=4 * seqs * rows * width_in * width_out,
            bytes_accessed=4 * (2 * seqs * rows * width + owners * 16 * width_in),
            transcendentals=0,
        ),
    )(tile_map.T, core, own, other)


def covariance_kernel(terms_ref, prior_ref, o_ref):
    blocks = jnp.sum(terms_ref[...], axis=0)
    left = jnp.concatenate([blocks[0:4], blocks[4:8]], axis=1)
    right = jnp.concatenate([blocks[8:12], blocks[12:16]], axis=1)
    product = lax.dot_general(
        left, right, (((0,), (0,)), ((), ())), precision=HIGHEST, preferred_element_type=jnp.float32
    )
    o_ref[0] = prior_ref[0] + product


def covariance(terms, prior_cov):
    return pl.pallas_call(
        covariance_kernel,
        out_shape=jax.ShapeDtypeStruct(prior_cov.shape, jnp.float32),
        in_specs=[pl.BlockSpec(memory_space=pltpu.VMEM)] * 2,
        out_specs=pl.BlockSpec(memory_space=pltpu.VMEM),
        compiler_params=pltpu.CompilerParams(vmem_limit_bytes=VMEM_LIMIT),
    )(terms, prior_cov)


def body(activations, out_grads, proj_in, proj_out, seq_lengths, tile_map, prior_cov):
    seqs, tok, _ = activations.shape
    width_in, width_out = proj_in.shape[1], proj_out.shape[1]
    pieces = lax.axis_size("tile")
    rows = tok // pieces
    width = width_in + width_out
    owners = lax.axis_size("y") * pieces
    partial = project(activations, out_grads, proj_in, proj_out, pieces)
    partial = partial.reshape(pieces, seqs * rows, width)
    arrived = lax.all_to_all(partial, "tile", 0, 0, tiled=True)
    summed = jnp.sum(arrived.reshape(pieces, seqs, rows, width), axis=0)
    core = lax.axis_index("core")
    positions = (
        (lax.axis_index("y") * 2 + core) * tok
        + lax.axis_index("tile") * rows
        + jnp.arange(rows, dtype=jnp.int32)
    )
    weight = jnp.where(
        positions[None, :] < seq_lengths[:, None],
        lax.rsqrt(seq_lengths.astype(jnp.float32))[:, None],
        0.0,
    )
    grad_side = lax.broadcasted_iota(jnp.int32, (1, 1, width), 2) >= width_in
    own = summed * jnp.where(grad_side, weight[:, :, None], 1.0)
    other = lax.ppermute(own, "core", [(0, 1), (1, 0)])
    terms = expand(tile_map, core.reshape(1).astype(jnp.int32), own, other, owners, width_in)
    terms = lax.all_to_all(terms, ("y", "tile"), 0, 0, tiled=True)
    return covariance(terms.reshape(owners, 16, width_in), prior_cov)


def solution(mesh):
    layers, seq, tile = (mesh.shape[name] for name in ("layer", "seq", "tile"))
    fine = Mesh(mesh.devices.reshape(layers, seq // 2, 2, tile), ("layer", "y", "core", "tile"))
    split = ("y", "core")
    return jax.shard_map(
        body,
        mesh=fine,
        in_specs=(
            P("layer", split, "tile"),
            P("layer", split, "tile"),
            P(("layer", "tile"), None),
            P(("layer", "tile"), None),
            P(),
            P(),
            P(("layer", "y", "core", "tile"), None, None),
        ),
        out_specs=P(("layer", "y", "core", "tile"), None, None),
        check_vma=False,
    )
```

time: 484 us -> 83.5 us (0.17)
  waiting for transfers between devices: 308 us -> 32.8 us
  blocking collectives: 137 us -> 27.2 us
  local copies, waits for them, and re-layouts: 18.5 us -> 5.01 us
  between operations: 13.5 us -> 0.09 us
  starting transfers between devices: 0.04 us -> 12.4 us
  matrix products: 5.56 us -> 0 us
  Pallas kernels: 0 us -> 5.16 us
    reduce_scatter x1 -> x0, waiting for transfers between devices: 221 us -> none  [body(): lax.psum_scatter(partial_value, ('seq', 'tile'), scatter_dimension=1, til...]
    all_gather x1 -> x0, blocking collectives: 137 us -> none  [body(): shard_piece = lax.all_gather(features, ('seq', 'tile'), axis=1, tiled=True)]
    psum x1 -> x0, waiting for transfers between devices: 86.7 us -> none  [body(): totals = lax.psum(whole_term, 'tile')]
    all_to_all x0 -> x1, waiting for transfers between devices: none -> 31.4 us  [body(): arrived = lax.all_to_all(partial, 'tile', 0, 0, tiled=True)]
    all_to_all x0 -> x1, blocking collectives: none -> 27.2 us  [body(): terms = lax.all_to_all(terms, ('y', 'tile'), 0, 0, tiled=True)]
    all_to_all x0 -> x1, starting transfers between devices: none -> 10.5 us  [body(): arrived = lax.all_to_all(partial, 'tile', 0, 0, tiled=True)]
    reshape x1 -> x0, local copies, waits for them, and re-layouts: 8.7 us -> none  [body(): partial_value = partial_value.reshape(seq_count, width_out * width_in)]
    gather x1 -> x0, local copies, waits for them, and re-layouts: 6.8 us -> none  [body(): jnp.take(shard_piece, jnp.clip(columns, 0, piece_width - 1), axis=1)]
where the time goes in v1:
time: 83.5 us; the launch traced here: 82.8 us
  waiting for transfers between devices  32.8 us (39%)
  blocking collectives  27.2 us (33%)
  starting transfers between devices  12.4 us (15%)
  Pallas kernels  5.16 us (6%)
  local copies, waits for them, and re-layouts  5.01 us (6%)
    all_to_all x1, waiting for transfers between devices, body(): arrived = lax.all_to_all(partial, 'tile', 0, 0, tiled=True)  31.4 us
    all_to_all x1, blocking collectives, body(): terms = lax.all_to_all(terms, ('y', 'tile'), 0, 0, tiled=True)  27.2 us
    all_to_all x1, starting transfers between devices, body(): arrived = lax.all_to_all(partial, 'tile', 0, 0, tiled=True)  10.5 us
    unnamed x14, local copies, waits for them, and re-layouts  5.01 us
    pallas_call x1, Pallas kernels, project(): pl.pallas_call(project_kernel, grid=(seqs,), out_shape=jax.ShapeDtypeStru...  2.63 us
    ppermute x1, starting transfers between devices, body(): other = lax.ppermute(own, 'core', [(0, 1), (1, 0)])  1.93 us
  transfers between devices with their start and end apart: 2, of which 2 were waited for; matrix products, arithmetic and copies ran while one was open for 0% of the time, Pallas kernels for 0%

profile of v1, /device:TPU:6, one launch (start us, length us, event | category | flops | bytes accessed | tf_op | source)
XLA Modules:
  0.0 82.8 jit_solution(3195745749628687442)
XLA Ops:
  0.0 0.0 copy-start
  0.0 1.8 %copy-done = bf16[4,192,1792]{2,1,0:T(8,128)(2,1)S(1)} copy-done((bf16[4,192,1792]{2,1,0:T(8,128)(2,1)S(1)}, bf16[4,192,1792]{2,1,0:T(8,128)(2,1)}, u32[]{:S(2)}) %copy-start) | copy-done | bytes 2752536
  1.8 0.0 copy-start.1
  1.8 1.2 %copy-done.1 = bf16[1792,256]{1,0:T(8,128)(2,1)S(1)} copy-done((bf16[1792,256]{1,0:T(8,128)(2,1)S(1)}, bf16[1792,256]{1,0:T(8,128)(2,1)}, u32[]{:S(2)}) %copy-start.1) | copy-done | bytes 917528
  3.0 0.0 copy-start.2
  3.0 1.1 %copy-done.2 = bf16[4,192,512]{2,1,0:T(8,128)(2,1)S(1)} copy-done((bf16[4,192,512]{2,1,0:T(8,128)(2,1)S(1)}, bf16[4,192,512]{2,1,0:T(8,128)(2,1)}, u32[]{:S(2)}) %copy-start.2) | copy-done | bytes 786456
  4.1 0.0 copy-start.4
  4.1 0.9 %copy-done.4 = bf16[512,128]{1,0:T(8,128)(2,1)S(1)} copy-done((bf16[512,128]{1,0:T(8,128)(2,1)S(1)}, bf16[512,128]{1,0:T(8,128)(2,1)}, u32[]{:S(2)}) %copy-start.4) | copy-done | bytes 131096
  5.0 2.6 %shard_map.73 = f32[8,4,24,384]{3,2,1,0:T(8,128)} custom-call(bf16[4,192,512]{2,1,0:T(8,128)(2,1)S(1)} %copy-done.2, bf16[4,192,1792]{2,1,0:T(8,128)(2,1)S(1)} %copy-done, bf16[512,128]{1,0:T(8,128)(2,1)S(1)} %copy-done.4, bf16[1792,256]{1,0:T(8,128)(2,1)S(1)} %copy-done.1), custom_call_target="tpu_custom_call" | custom-call | flops 805306368 | bytes 4718592 | tf_op jit(solution)/shard_map/pallas_call | solution.py:29
  7.6 0.0 copy-start.6
  7.6 10.5 %all-to-all-start = ((f32[8,96,384]{2,1,0:T(8,128)}), f32[8,96,384]{2,1,0:T(8,128)S(1)}, u32[]{:S(2)}, u32[]{:S(2)}) async-start(f32[8,96,384]{2,1,0:T(8,128)} %bitcast.2), calls=%async_computation | async-start | bytes 2359296 | tf_op jit(solution)/shard_map/all_to_all | solution.py:122
  18.1 0.0 copy-done.6
  18.1 0.1 compare_select_fusion
  18.2 31.4 %all-to-all-done = f32[8,96,384]{2,1,0:T(8,128)S(1)} async-done(((f32[8,96,384]{2,1,0:T(8,128)}), f32[8,96,384]{2,1,0:T(8,128)S(1)}, u32[]{:S(2)}, u32[]{:S(2)}) %all-to-all-start) | async-done | bytes 1179680 | tf_op jit(solution)/shard_map/all_to_all | solution.py:122
  49.7 0.1 reduce_sum.11
  49.7 0.0 copy-start.3
  49.7 0.1 select_multiply_fusion.own_ref
  49.8 1.9 %collective-permute-start = (f32[4,24,384]{2,1,0:T(8,128)S(1)}, f32[4,24,384]{2,1,0:T(8,128)S(1)}, u32[]{:S(2)}, u32[]{:S(2)}) collective-permute-start(f32[4,24,384]{2,1,0:T(8,128)S(1)} %select_multiply_fusion.own_ref), channel_id=1, source_target_pairs={{0,8},{8,0},{1,9},{9,1},{2,10},{10,2},{3,11},{11,3},{4,12},{12,4},... | collective-permute-start | bytes 442376 | tf_op jit(solution)/shard_map/ppermute | solution.py:137
  51.8 1.3 %collective-permute-done.other_ref = f32[4,24,384]{2,1,0:T(8,128)S(1)} collective-permute-done((f32[4,24,384]{2,1,0:T(8,128)S(1)}, f32[4,24,384]{2,1,0:T(8,128)S(1)}, u32[]{:S(2)}, u32[]{:S(2)}) %collective-permute-start) | collective-permute-done | bytes 147488 | tf_op jit(solution)/shard_map/ppermute | solution.py:137
  53.1 0.0 copy-done.5
  53.1 1.3 %shard_map.74 = f32[1024,128]{1,0:T(8,128)S(1)} custom-call(s32[2,128]{1,0:T(2,128)S(1)} %bitcast.6, s32[1]{0:T(128)} %bitcast.1.core_ref, f32[4,24,384]{2,1,0:T(8,128)S(1)} %select_multiply_fusion.own_ref, f32[4,24,384]{2,1,0:T(8,128)S(1)} %collective-permute-done.other_ref), custom_call_target="tpu_custom_call" | custom-call | flops 12582912 | bytes 819200 | tf_op jit(solution)/shard_map/pallas_call | solution.py:73
  54.4 27.2 %all_to_all.14.terms_ref = f32[64,16,128]{2,1,0:T(8,128)S(1)} all-to-all(f32[64,16,128]{2,1,0:T(8,128)S(1)} %bitcast.5), channel_id=1, replica_groups=mesh['layer'=4,'y'=8,'core'=2,'tile'=8] {'y','tile'}, dimensions={0} | all-to-all | bytes 1048576 | tf_op jit(solution)/shard_map/all_to_all | solution.py:139
  81.6 0.0 copy-done.3
  81.6 1.2 %shard_map.75 = f32[1,256,256]{2,1,0:T(8,128)} custom-call(f32[64,16,128]{2,1,0:T(8,128)S(1)} %all_to_all.14.terms_ref, f32[1,256,256]{2,1,0:T(8,128)S(1)} %copy-done.3), custom_call_target="tpu_custom_call" | custom-call | tf_op jit(solution)/shard_map/pallas_call | solution.py:104
  (4 shorter events, 0.0 us)
Async XLA Ops:
  0.0 1.8 %copy-start = (bf16[4,192,1792]{2,1,0:T(8,128)(2,1)S(1)}, bf16[4,192,1792]{2,1,0:T(8,128)(2,1)}, u32[]{:S(2)}) copy-start(bf16[4,192,1792]{2,1,0:T(8,128)(2,1)} %grad_ref.1) | copy-start | bytes 8257540
  1.8 1.2 %copy-start.1 = (bf16[1792,256]{1,0:T(8,128)(2,1)S(1)}, bf16[1792,256]{1,0:T(8,128)(2,1)}, u32[]{:S(2)}) copy-start(bf16[1792,256]{1,0:T(8,128)(2,1)} %out_ref.1) | copy-start | bytes 2752516
  3.0 1.1 %copy-start.2 = (bf16[4,192,512]{2,1,0:T(8,128)(2,1)S(1)}, bf16[4,192,512]{2,1,0:T(8,128)(2,1)}, u32[]{:S(2)}) copy-start(bf16[4,192,512]{2,1,0:T(8,128)(2,1)} %act_ref.1) | copy-start | bytes 2359300
  4.1 0.9 %copy-start.4 = (bf16[512,128]{1,0:T(8,128)(2,1)S(1)}, bf16[512,128]{1,0:T(8,128)(2,1)}, u32[]{:S(2)}) copy-start(bf16[512,128]{1,0:T(8,128)(2,1)} %in_ref.1) | copy-start | bytes 393220
  7.6 10.5 %copy-start.6 = (s32[4]{0:T(128)S(1)}, s32[4]{0:T(128)}, u32[]{:S(2)}) copy-start(s32[4]{0:T(128)} %param.11) | copy-start | bytes 52
  7.6 42.0 %all-to-all-start = ((f32[8,96,384]{2,1,0:T(8,128)}), f32[8,96,384]{2,1,0:T(8,128)S(1)}, u32[]{:S(2)}, u32[]{:S(2)}) async-start(f32[8,96,384]{2,1,0:T(8,128)} %bitcast.2), calls=%async_computation | async-start | bytes 2359296 | tf_op jit(solution)/shard_map/all_to_all | solution.py:122
  18.1 35.0 %copy-start.5 = (s32[128,2]{0,1:T(2,128)S(1)}, s32[128,2]{0,1:T(2,128)}, u32[]{:S(2)}) copy-start(s32[128,2]{0,1:T(2,128)} %param.12) | copy-start | bytes 3076
  49.7 31.9 %copy-start.3 = (f32[1,256,256]{2,1,0:T(8,128)S(1)}, f32[1,256,256]{2,1,0:T(8,128)}, u32[]{:S(2)}) copy-start(f32[1,256,256]{2,1,0:T(8,128)} %prior_ref.1) | copy-start | bytes 786436
  49.8 3.3 %collective-permute-start = (f32[4,24,384]{2,1,0:T(8,128)S(1)}, f32[4,24,384]{2,1,0:T(8,128)S(1)}, u32[]{:S(2)}, u32[]{:S(2)}) collective-permute-start(f32[4,24,384]{2,1,0:T(8,128)S(1)} %select_multiply_fusion.own_ref), channel_id=1, source_target_pairs={{0,8},{8,0},{1,9},{9,1},{2,10},{10,2},{3,11},{11,3},{4,12},{12,4},... | collective-permute-start | bytes 442376 | tf_op jit(solution)/shard_map/ppermute | solution.py:137

commit v2 on v1

v2 whole, which is shorter than its diff:
```python
import jax
import jax.numpy as jnp
from jax import lax
from jax.experimental import pallas as pl
from jax.experimental.pallas import tpu as pltpu
from jax.sharding import Mesh
from jax.sharding import PartitionSpec as P

HIGHEST = lax.Precision.HIGHEST
VMEM_LIMIT = 4 * 1024 * 1024
PROJECT_VMEM = 8 * 1024 * 1024


def project_kernel(x_ref, w_ref, o_ref):
    product = jnp.dot(x_ref[0], w_ref[...], preferred_element_type=jnp.float32)
    o_ref[...] = product


def project(x, w):
    seqs, tok, dim = x.shape
    width = w.shape[1]
    return pl.pallas_call(
        project_kernel,
        grid=(seqs,),
        out_shape=jax.ShapeDtypeStruct((seqs * tok, width), jnp.float32),
        in_specs=[
            pl.BlockSpec((1, tok, dim), lambda s: (s, 0, 0)),
            pl.BlockSpec((dim, width), lambda s: (0, 0)),
        ],
        out_specs=pl.BlockSpec((tok, width), lambda s: (s, 0)),
        compiler_params=pltpu.CompilerParams(vmem_limit_bytes=PROJECT_VMEM),
        cost_estimate=pl.CostEstimate(
            flops=2 * seqs * tok * dim * width,
            bytes_accessed=2 * seqs * tok * dim + 4 * seqs * tok * width,
            transcendentals=0,
        ),
    )(x, w)


def combine_kernel(terms_ref, weight_ref, right_ref, o_ref, held_ref):
    own = jnp.sum(terms_ref[...], axis=0) * weight_ref[...]
    for piece in range(o_ref.shape[0]):
        o_ref[piece] = own


def combine(terms, weight, right):
    return pl.pallas_call(
        combine_kernel,
        out_shape=(
            jax.ShapeDtypeStruct(terms.shape, jnp.float32),
            jax.ShapeDtypeStruct(right.shape, jnp.float32),
        ),
        in_specs=[pl.BlockSpec(memory_space=pltpu.VMEM)] * 3,
        out_specs=(pl.BlockSpec(memory_space=pltpu.VMEM),) * 2,
        input_output_aliases={2: 1},
        compiler_params=pltpu.CompilerParams(vmem_limit_bytes=VMEM_LIMIT),
    )(terms, weight, right)


def outer_kernel(left_ref, right_ref, o_ref):
    seqs, _, width_out = right_ref.shape
    for s in range(seqs):
        o_ref[pl.ds(s, width_out, stride=seqs), :] = lax.dot_general(
            right_ref[s], left_ref[s], (((0,), (0,)), ((), ())), precision=HIGHEST, preferred_element_type=jnp.float32
        )


def outer(left, right):
    seqs, _, width_in = left.shape
    width_out = right.shape[2]
    return pl.pallas_call(
        outer_kernel,
        out_shape=jax.ShapeDtypeStruct((seqs * width_out, width_in), jnp.float32),
        in_specs=[pl.BlockSpec(memory_space=pltpu.VMEM)] * 2,
        out_specs=pl.BlockSpec(memory_space=pltpu.VMEM),
        compiler_params=pltpu.CompilerParams(vmem_limit_bytes=VMEM_LIMIT),
    )(left, right)


def expand_kernel(map_ref, core_ref, own_ref, other_ref, o_ref):
    core = core_ref[0]
    owners = o_ref.shape[0] // 16
    for n in range(owners):
        k = (2 * (n // 8) + core) * 8 + n % 8
        for side in range(2):
            at = pl.ds(pl.multiple_of(map_ref[side, k] * 8, 8), 8)
            o_ref[16 * n + 8 * side:16 * n + 8 * side + 8, :] = own_ref[at, :] + other_ref[at, :]


def expand(tile_map, core, own, other, owners):
    return pl.pallas_call(
        expand_kernel,
        out_shape=jax.ShapeDtypeStruct((owners * 16, own.shape[1]), jnp.float32),
        in_specs=[
            pl.BlockSpec(memory_space=pltpu.SMEM),
            pl.BlockSpec(memory_space=pltpu.SMEM),
            pl.BlockSpec(memory_space=pltpu.VMEM),
            pl.BlockSpec(memory_space=pltpu.VMEM),
        ],
        out_specs=pl.BlockSpec(memory_space=pltpu.VMEM),
        compiler_params=pltpu.CompilerParams(vmem_limit_bytes=VMEM_LIMIT),
    )(tile_map.T, core, own, other)


def covariance_kernel(terms_ref, prior_ref, o_ref):
    blocks = jnp.sum(terms_ref[...], axis=0)
    left = jnp.concatenate([blocks[0:4], blocks[4:8]], axis=1)
    right = jnp.concatenate([blocks[8:12], blocks[12:16]], axis=1)
    product = lax.dot_general(
        left, right, (((0,), (0,)), ((), ())), precision=HIGHEST, preferred_element_type=jnp.float32
    )
    o_ref[0] = prior_ref[0] + product


def covariance(terms, prior_cov):
    return pl.pallas_call(
        covariance_kernel,
        out_shape=jax.ShapeDtypeStruct(prior_cov.shape, jnp.float32),
        in_specs=[pl.BlockSpec(memory_space=pltpu.VMEM)] * 2,
        out_specs=pl.BlockSpec(memory_space=pltpu.VMEM),
        compiler_params=pltpu.CompilerParams(vmem_limit_bytes=VMEM_LIMIT),
    )(terms, prior_cov)


def body(activations, out_grads, proj_in, proj_out, seq_lengths, tile_map, prior_cov):
    seqs, tok, _ = activations.shape
    width_in = proj_in.shape[1]
    pieces = lax.axis_size("tile")
    rows = seqs * tok // pieces
    owners = lax.axis_size("y") * pieces
    left = jnp.dot(activations.reshape(seqs * tok, -1), proj_in, preferred_element_type=jnp.float32)
    arrived = lax.all_to_all(left.reshape(pieces, rows, width_in), "tile", 0, 0, tiled=True)
    right = project(out_grads, proj_out)
    core = lax.axis_index("core")
    token = lax.axis_index("tile") * rows + jnp.arange(rows, dtype=jnp.int32)
    position = (lax.axis_index("y") * 2 + core) * tok + token % tok
    length = jnp.sum(jnp.where(token[:, None] // tok == jnp.arange(seqs)[None, :], seq_lengths[None, :], 0), axis=1)
    weight = jnp.where(position < length, lax.rsqrt(length.astype(jnp.float32)), 0.0)
    weight = jnp.broadcast_to(weight[:, None], (rows, width_in))
    arrived, right, weight = lax.optimization_barrier((arrived, right, weight))
    copies, right = combine(arrived, weight, right)
    left = lax.all_to_all(copies, "tile", 0, 0, tiled=True).reshape(seqs, tok, width_in)
    right = right.reshape(seqs, tok, -1)
    grads = outer(left, right)
    other = lax.ppermute(grads, "core", [(0, 1), (1, 0)])
    terms = expand(tile_map, core.reshape(1).astype(jnp.int32), grads, other, owners)
    terms = lax.all_to_all(terms.reshape(owners, 16, width_in), ("y", "tile"), 0, 0, tiled=True)
    return covariance(terms, prior_cov)


def solution(mesh):
    layers, seq, tile = (mesh.shape[name] for name in ("layer", "seq", "tile"))
    fine = Mesh(mesh.devices.reshape(layers, seq // 2, 2, tile), ("layer", "y", "core", "tile"))
    split = ("y", "core")
    return jax.shard_map(
        body,
        mesh=fine,
        in_specs=(
            P("layer", split, "tile"),
            P("layer", split, "tile"),
            P(("layer", "tile"), None),
            P(("layer", "tile"), None),
            P(),
            P(),
            P(("layer", "y", "core", "tile"), None, None),
        ),
        out_specs=P(("layer", "y", "core", "tile"), None, None),
        check_vma=False,
    )
```

time: 83.5 us -> 79.9 us (0.957)
  waiting for transfers between devices: 32.8 us -> 13.2 us
  blocking collectives: 27.2 us -> 43.9 us
  matrix products: 0 us -> 2.01 us
  local copies, waits for them, and re-layouts: 5.01 us -> 3 us
    all_to_all x1, waiting for transfers between devices: 31.4 us -> 11.3 us  [body(): lax.all_to_all(left.reshape(pieces, rows, width_in), 'tile', 0, 0, tiled=...]
    all_to_all x1 -> x2, blocking collectives: 27.2 us -> 43.9 us  [the longest x1 27.2 us: body(): lax.all_to_all(terms.reshape(owners, 16, width_in), ('y', 'tile'), 0, 0,...]
    unnamed x14 -> x12, local copies, waits for them, and re-layouts: 5.01 us -> 2.92 us
    dot_general x0 -> x1, matrix products: none -> 2.01 us  [body(): jnp.dot(activations.reshape(seqs * tok, -1), proj_in, preferred_element_t...]
    pallas_call x1, Pallas kernels: 2.63 us -> 1.43 us  [project(): pl.pallas_call(project_kernel, grid=(seqs,), out_shape=jax.ShapeDtypeStru...]
    pallas_call x0 -> x2, Pallas kernels: none -> 1.15 us  [the longest x1 1.11 us: outer(): pl.pallas_call(outer_kernel, out_shape=jax.ShapeDtypeStruct((seqs * width...]
  transfers between devices with their start and end apart: 2 -> 2, of which waited for: 2 -> 2; matrix products, arithmetic and copies ran while one was open for 0% -> 0% of each run, Pallas kernels for 0% -> 2%
where the time goes in v2:
time: 79.9 us; the launch traced here: 79.2 us
  blocking collectives  43.9 us (55%)
  waiting for transfers between devices  13.2 us (17%)
  starting transfers between devices  12.4 us (16%)
  Pallas kernels  4.56 us (6%)
  local copies, waits for them, and re-layouts  3 us (4%)
  matrix products  2.01 us (3%)
    all_to_all x1, blocking collectives, body(): lax.all_to_all(terms.reshape(owners, 16, width_in), ('y', 'tile'), 0, 0,...  27.2 us
    all_to_all x1, blocking collectives, body(): lax.all_to_all(copies, 'tile', 0, 0, tiled=True)  16.7 us
    all_to_all x1, waiting for transfers between devices, body(): lax.all_to_all(left.reshape(pieces, rows, width_in), 'tile', 0, 0, tiled=...  11.3 us
    all_to_all x1, starting transfers between devices, body(): lax.all_to_all(left.reshape(pieces, rows, width_in), 'tile', 0, 0, tiled=...  10.5 us
    unnamed x12, local copies, waits for them, and re-layouts  2.92 us
    dot_general x1, matrix products, body(): jnp.dot(activations.reshape(seqs * tok, -1), proj_in, preferred_element_t...  2.01 us
    ppermute x1, starting transfers between devices, body(): other = lax.ppermute(grads, 'core', [(0, 1), (1, 0)])  1.92 us
    ppermute x1, waiting for transfers between devices, body(): other = lax.ppermute(grads, 'core', [(0, 1), (1, 0)])  1.88 us
  transfers between devices with their start and end apart: 2, of which 2 were waited for; matrix products, arithmetic and copies ran while one was open for 0% of the time, Pallas kernels for 2%

profile of v2, /device:TPU:6, one launch (start us, length us, event | category | flops | bytes accessed | tf_op | source)
XLA Modules:
  0.0 79.2 jit_solution(708700714108286770)
XLA Ops:
  0.0 0.0 copy-start
  0.0 0.0 copy-start.2
  0.0 1.1 %copy-done = bf16[4,192,512]{2,1,0:T(8,128)(2,1)S(1)} copy-done((bf16[4,192,512]{2,1,0:T(8,128)(2,1)S(1)}, bf16[4,192,512]{2,1,0:T(8,128)(2,1)}, u32[]{:S(2)}) %copy-start) | copy-done | bytes 786456
  1.1 2.0 %fusion = f32[8,96,128]{2,1,0:T(8,128)} fusion(bf16[8,96,512]{2,1,0:T(8,128)(2,1)S(1)} %bitcast.10, bf16[512,128]{1,0:T(8,128)(2,1)} %param.9), kind=kOutput, calls=%fused_computation | convolution fusion | flops 100663296 | bytes 1310720 | tf_op jit(solution)/shard_map/dot_general | solution.py:131
  3.1 10.5 %all-to-all-start = ((f32[8,96,128]{2,1,0:T(8,128)}), f32[8,96,128]{2,1,0:T(8,128)S(1)}, u32[]{:S(2)}, u32[]{:S(2)}) async-start(f32[8,96,128]{2,1,0:T(8,128)} %fusion), calls=%async_computation | async-start | bytes 786432 | tf_op jit(solution)/shard_map/all_to_all | solution.py:132
  13.6 0.0 copy-done.2
  13.6 0.0 copy-start.1
  13.6 1.8 %copy-done.1 = bf16[4,192,1792]{2,1,0:T(8,128)(2,1)S(1)} copy-done((bf16[4,192,1792]{2,1,0:T(8,128)(2,1)S(1)}, bf16[4,192,1792]{2,1,0:T(8,128)(2,1)}, u32[]{:S(2)}) %copy-start.1) | copy-done | bytes 2752536
  15.4 1.4 %shard_map.73.right_ref = f32[768,256]{1,0:T(8,128)S(1)} custom-call(bf16[4,192,1792]{2,1,0:T(8,128)(2,1)S(1)} %copy-done.1, bf16[1792,256]{1,0:T(8,128)(2,1)S(1)} %copy-done.2), custom_call_target="tpu_custom_call" | custom-call | flops 704643072 | bytes 3538944 | tf_op jit(solution)/shard_map/pallas_call | solution.py:22
  16.8 0.0 copy-start.4
  16.9 0.0 copy-done.5
  16.9 0.1 select_reduce_fusion
  17.0 11.3 %all-to-all-done.terms_ref = f32[8,96,128]{2,1,0:T(8,128)S(1)} async-done(((f32[8,96,128]{2,1,0:T(8,128)}), f32[8,96,128]{2,1,0:T(8,128)S(1)}, u32[]{:S(2)}, u32[]{:S(2)}) %all-to-all-start) | async-done | bytes 393248 | tf_op jit(solution)/shard_map/all_to_all | solution.py:132
  28.3 0.1 broadcast_in_dim.28.weight_ref
  28.4 0.0 copy-start.3
  28.4 16.7 %all_to_all.15 = f32[8,96,128]{2,1,0:T(8,128)S(1)} all-to-all(f32[8,96,128]{2,1,0:T(8,128)S(1)} %get-tuple-element.13), channel_id=1, replica_groups=mesh['layer'=4,'y'=8,'core'=2,'tile'=8] {'tile'}, dimensions={0} | all-to-all | bytes 786432 | tf_op jit(solution)/shard_map/all_to_all | solution.py:142
  45.1 1.1 %shard_map.75.own_ref = f32[1024,128]{1,0:T(8,128)S(1)} custom-call(f32[4,192,128]{2,1,0:T(8,128)S(1)} %bitcast.13, f32[4,192,256]{2,1,0:T(8,128)S(1)} %bitcast.11), custom_call_target="tpu_custom_call" | custom-call | tf_op jit(solution)/shard_map/pallas_call | solution.py:71
  46.2 1.9 %collective-permute-start = (f32[1024,128]{1,0:T(8,128)S(1)}, f32[1024,128]{1,0:T(8,128)S(1)}, u32[]{:S(2)}, u32[]{:S(2)}) collective-permute-start(f32[1024,128]{1,0:T(8,128)S(1)} %shard_map.75.own_ref), channel_id=1, source_target_pairs={{0,8},{8,0},{1,9},{9,1},{2,10},{10,2},{3,11},{11,3},{4,12},{12,4},... | collective-permute-start | bytes 1572872 | tf_op jit(solution)/shard_map/ppermute | solution.py:145
  48.2 1.9 %collective-permute-done.other_ref = f32[1024,128]{1,0:T(8,128)S(1)} collective-permute-done((f32[1024,128]{1,0:T(8,128)S(1)}, f32[1024,128]{1,0:T(8,128)S(1)}, u32[]{:S(2)}, u32[]{:S(2)}) %collective-permute-start) | collective-permute-done | bytes 524320 | tf_op jit(solution)/shard_map/ppermute | solution.py:145
  50.0 0.0 copy-done.4
  50.0 0.8 shard_map.76
  50.8 27.2 %all_to_all.16.terms_ref = f32[64,16,128]{2,1,0:T(8,128)S(1)} all-to-all(f32[64,16,128]{2,1,0:T(8,128)S(1)} %bitcast.12), channel_id=1, replica_groups=mesh['layer'=4,'y'=8,'core'=2,'tile'=8] {'y','tile'}, dimensions={0} | all-to-all | bytes 1048576 | tf_op jit(solution)/shard_map/all_to_all | solution.py:147
  78.1 0.0 copy-done.3
  78.1 1.2 %shard_map.77 = f32[1,256,256]{2,1,0:T(8,128)} custom-call(f32[64,16,128]{2,1,0:T(8,128)S(1)} %all_to_all.16.terms_ref, f32[1,256,256]{2,1,0:T(8,128)S(1)} %copy-done.3), custom_call_target="tpu_custom_call" | custom-call | tf_op jit(solution)/shard_map/pallas_call | solution.py:116
  (4 shorter events, 0.1 us)
Async XLA Ops:
  0.0 1.1 %copy-start = (bf16[4,192,512]{2,1,0:T(8,128)(2,1)S(1)}, bf16[4,192,512]{2,1,0:T(8,128)(2,1)}, u32[]{:S(2)}) copy-start(bf16[4,192,512]{2,1,0:T(8,128)(2,1)} %param.7) | copy-start | bytes 2359300
  0.0 13.6 %copy-start.2 = (bf16[1792,256]{1,0:T(8,128)(2,1)S(1)}, bf16[1792,256]{1,0:T(8,128)(2,1)}, u32[]{:S(2)}) copy-start(bf16[1792,256]{1,0:T(8,128)(2,1)} %w_ref.1) | copy-start | bytes 2752516
  3.1 13.7 %copy-start.5 = (s32[4]{0:T(128)S(1)}, s32[4]{0:T(128)}, u32[]{:S(2)}) copy-start(s32[4]{0:T(128)} %param.11) | copy-start | bytes 52
  3.1 25.1 %all-to-all-start = ((f32[8,96,128]{2,1,0:T(8,128)}), f32[8,96,128]{2,1,0:T(8,128)S(1)}, u32[]{:S(2)}, u32[]{:S(2)}) async-start(f32[8,96,128]{2,1,0:T(8,128)} %fusion), calls=%async_computation | async-start | bytes 786432 | tf_op jit(solution)/shard_map/all_to_all | solution.py:132
  13.6 1.8 %copy-start.1 = (bf16[4,192,1792]{2,1,0:T(8,128)(2,1)S(1)}, bf16[4,192,1792]{2,1,0:T(8,128)(2,1)}, u32[]{:S(2)}) copy-start(bf16[4,192,1792]{2,1,0:T(8,128)(2,1)} %x_ref.1) | copy-start | bytes 8257540
  16.8 33.2 %copy-start.4 = (s32[128,2]{0,1:T(2,128)S(1)}, s32[128,2]{0,1:T(2,128)}, u32[]{:S(2)}) copy-start(s32[128,2]{0,1:T(2,128)} %param.12) | copy-start | bytes 3076
  28.4 49.7 %copy-start.3 = (f32[1,256,256]{2,1,0:T(8,128)S(1)}, f32[1,256,256]{2,1,0:T(8,128)}, u32[]{:S(2)}) copy-start(f32[1,256,256]{2,1,0:T(8,128)} %prior_ref.1) | copy-start | bytes 786436
  46.2 3.8 %collective-permute-start = (f32[1024,128]{1,0:T(8,128)S(1)}, f32[1024,128]{1,0:T(8,128)S(1)}, u32[]{:S(2)}, u32[]{:S(2)}) collective-permute-start(f32[1024,128]{1,0:T(8,128)S(1)} %shard_map.75.own_ref), channel_id=1, source_target_pairs={{0,8},{8,0},{1,9},{9,1},{2,10},{10,2},{3,11},{11,3},{4,12},{12,4},... | collective-permute-start | bytes 1572872 | tf_op jit(solution)/shard_map/ppermute | solution.py:145

commit v3 on v2

--- a/solution.py
+++ b/solution.py
@@ -1,3 +1,5 @@
+import functools
+
 import jax
 import jax.numpy as jnp
 from jax import lax
@@ -6,7 +8,6 @@
 from jax.sharding import Mesh
 from jax.sharding import PartitionSpec as P
 
-HIGHEST = lax.Precision.HIGHEST
 VMEM_LIMIT = 4 * 1024 * 1024
 PROJECT_VMEM = 8 * 1024 * 1024
 
@@ -57,11 +58,21 @@
     )(terms, weight, right)
 
 
+def high_and_rest(x):
+    high = x.astype(jnp.bfloat16)
+    return high, (x - high.astype(jnp.float32)).astype(jnp.bfloat16)
+
+
 def outer_kernel(left_ref, right_ref, o_ref):
     seqs, _, width_out = right_ref.shape
     for s in range(seqs):
+        left_high, left_rest = high_and_rest(left_ref[s])
+        right_high, right_rest = high_and_rest(right_ref[s])
         o_ref[pl.ds(s, width_out, stride=seqs), :] = lax.dot_general(
-            right_ref[s], left_ref[s], (((0,), (0,)), ((), ())), precision=HIGHEST, preferred_element_type=jnp.float32
+            jnp.concatenate([right_high, right_high, right_rest], axis=0),
+            jnp.concatenate([left_high, left_rest, left_high], axis=0),
+            (((0,), (0,)), ((), ())),
+            preferred_element_type=jnp.float32,
         )
 
 
@@ -77,19 +88,20 @@
     )(left, right)
 
 
-def expand_kernel(map_ref, core_ref, own_ref, other_ref, o_ref):
+def expand_kernel(chips, map_ref, core_ref, own_ref, other_ref, o_ref):
     core = core_ref[0]
     owners = o_ref.shape[0] // 16
+    pieces = owners // chips
     for n in range(owners):
-        k = (2 * (n // 8) + core) * 8 + n % 8
+        k = (2 * (n % chips) + core) * pieces + n // chips
         for side in range(2):
             at = pl.ds(pl.multiple_of(map_ref[side, k] * 8, 8), 8)
             o_ref[16 * n + 8 * side:16 * n + 8 * side + 8, :] = own_ref[at, :] + other_ref[at, :]
 
 
-def expand(tile_map, core, own, other, owners):
+def expand(tile_map, core, own, other, owners, chips):
     return pl.pallas_call(
-        expand_kernel,
+        functools.partial(expand_kernel, chips),
         out_shape=jax.ShapeDtypeStruct((owners * 16, own.shape[1]), jnp.float32),
         in_specs=[
             pl.BlockSpec(memory_space=pltpu.SMEM),
@@ -106,8 +118,13 @@
     blocks = jnp.sum(terms_ref[...], axis=0)
     left = jnp.concatenate([blocks[0:4], blocks[4:8]], axis=1)
     right = jnp.concatenate([blocks[8:12], blocks[12:16]], axis=1)
+    left_high, left_rest = high_and_rest(left)
+    right_high, right_rest = high_and_rest(right)
     product = lax.dot_general(
-        left, right, (((0,), (0,)), ((), ())), precision=HIGHEST, preferred_element_type=jnp.float32
+        jnp.concatenate([left_high, left_high, left_rest], axis=0),
+        jnp.concatenate([right_high, right_rest, right_high], axis=0),
+        (((0,), (0,)), ((), ())),
+        preferred_element_type=jnp.float32,
     )
     o_ref[0] = prior_ref[0] + product
 
@@ -143,8 +160,8 @@
     right = right.reshape(seqs, tok, -1)
     grads = outer(left, right)
     other = lax.ppermute(grads, "core", [(0, 1), (1, 0)])
-    terms = expand(tile_map, core.reshape(1).astype(jnp.int32), grads, other, owners)
-    terms = lax.all_to_all(terms.reshape(owners, 16, width_in), ("y", "tile"), 0, 0, tiled=True)
+    terms = expand(tile_map, core.reshape(1).astype(jnp.int32), grads, other, owners, lax.axis_size("y"))
+    terms = lax.all_to_all(terms.reshape(owners, 16, width_in), ("tile", "y"), 0, 0, tiled=True)
     return covariance(terms, prior_cov)
 
 

time: 79.9 us -> 79.5 us (level)
  no operation moved by 1% of the time
where the time goes in v3:
time: 79.5 us; the launch traced here: 79.1 us
  blocking collectives  44.5 us (56%)
  waiting for transfers between devices  13.2 us (17%)
  starting transfers between devices  12.4 us (16%)
  Pallas kernels  3.81 us (5%)
  local copies, waits for them, and re-layouts  3 us (4%)
  matrix products  2.01 us (3%)
    all_to_all x1, blocking collectives, body(): lax.all_to_all(terms.reshape(owners, 16, width_in), ('tile', 'y'), 0, 0,...  27.8 us
    all_to_all x1, blocking collectives, body(): lax.all_to_all(copies, 'tile', 0, 0, tiled=True)  16.7 us
    all_to_all x1, waiting for transfers between devices, body(): lax.all_to_all(left.reshape(pieces, rows, width_in), 'tile', 0, 0, tiled=...  11.3 us
    all_to_all x1, starting transfers between devices, body(): lax.all_to_all(left.reshape(pieces, rows, width_in), 'tile', 0, 0, tiled=...  10.5 us
    unnamed x12, local copies, waits for them, and re-layouts  2.92 us
    dot_general x1, matrix products, body(): jnp.dot(activations.reshape(seqs * tok, -1), proj_in, preferred_element_t...  2.01 us
    ppermute x1, starting transfers between devices, body(): other = lax.ppermute(grads, 'core', [(0, 1), (1, 0)])  1.92 us
    ppermute x1, waiting for transfers between devices, body(): other = lax.ppermute(grads, 'core', [(0, 1), (1, 0)])  1.88 us
  transfers between devices with their start and end apart: 2, of which 2 were waited for; matrix products, arithmetic and copies ran while one was open for 0% of the time, Pallas kernels for 2%

profile of v3, /device:TPU:6, one launch (start us, length us, event | category | flops | bytes accessed | tf_op | source)
XLA Modules:
  0.0 79.1 jit_solution(432358609874918455)
XLA Ops:
  0.0 0.0 copy-start
  0.0 0.0 copy-start.2
  0.0 1.1 %copy-done = bf16[4,192,512]{2,1,0:T(8,128)(2,1)S(1)} copy-done((bf16[4,192,512]{2,1,0:T(8,128)(2,1)S(1)}, bf16[4,192,512]{2,1,0:T(8,128)(2,1)}, u32[]{:S(2)}) %copy-start) | copy-done | bytes 786456
  1.1 2.0 %fusion = f32[8,96,128]{2,1,0:T(8,128)} fusion(bf16[8,96,512]{2,1,0:T(8,128)(2,1)S(1)} %bitcast.10, bf16[512,128]{1,0:T(8,128)(2,1)} %param.9), kind=kOutput, calls=%fused_computation | convolution fusion | flops 100663296 | bytes 1310720 | tf_op jit(solution)/shard_map/dot_general | solution.py:148
  3.1 10.5 %all-to-all-start = ((f32[8,96,128]{2,1,0:T(8,128)}), f32[8,96,128]{2,1,0:T(8,128)S(1)}, u32[]{:S(2)}, u32[]{:S(2)}) async-start(f32[8,96,128]{2,1,0:T(8,128)} %fusion), calls=%async_computation | async-start | bytes 786432 | tf_op jit(solution)/shard_map/all_to_all | solution.py:149
  13.6 0.0 copy-done.2
  13.6 0.0 copy-start.1
  13.6 1.8 %copy-done.1 = bf16[4,192,1792]{2,1,0:T(8,128)(2,1)S(1)} copy-done((bf16[4,192,1792]{2,1,0:T(8,128)(2,1)S(1)}, bf16[4,192,1792]{2,1,0:T(8,128)(2,1)}, u32[]{:S(2)}) %copy-start.1) | copy-done | bytes 2752536
  15.4 1.4 %shard_map.73.right_ref = f32[768,256]{1,0:T(8,128)S(1)} custom-call(bf16[4,192,1792]{2,1,0:T(8,128)(2,1)S(1)} %copy-done.1, bf16[1792,256]{1,0:T(8,128)(2,1)S(1)} %copy-done.2), custom_call_target="tpu_custom_call" | custom-call | flops 704643072 | bytes 3538944 | tf_op jit(solution)/shard_map/pallas_call | solution.py:23
  16.8 0.0 copy-start.4
  16.9 0.0 copy-done.5
  16.9 0.1 select_reduce_fusion
  17.0 11.3 %all-to-all-done.terms_ref = f32[8,96,128]{2,1,0:T(8,128)S(1)} async-done(((f32[8,96,128]{2,1,0:T(8,128)}), f32[8,96,128]{2,1,0:T(8,128)S(1)}, u32[]{:S(2)}, u32[]{:S(2)}) %all-to-all-start) | async-done | bytes 393248 | tf_op jit(solution)/shard_map/all_to_all | solution.py:149
  28.3 0.1 broadcast_in_dim.28.weight_ref
  28.4 0.0 copy-start.3
  28.4 16.7 %all_to_all.15 = f32[8,96,128]{2,1,0:T(8,128)S(1)} all-to-all(f32[8,96,128]{2,1,0:T(8,128)S(1)} %get-tuple-element.13), channel_id=1, replica_groups=mesh['layer'=4,'y'=8,'core'=2,'tile'=8] {'tile'}, dimensions={0} | all-to-all | bytes 786432 | tf_op jit(solution)/shard_map/all_to_all | solution.py:159
  45.1 0.5 shard_map.75.own_ref
  45.7 1.9 %collective-permute-start = (f32[1024,128]{1,0:T(8,128)S(1)}, f32[1024,128]{1,0:T(8,128)S(1)}, u32[]{:S(2)}, u32[]{:S(2)}) collective-permute-start(f32[1024,128]{1,0:T(8,128)S(1)} %shard_map.75.own_ref), channel_id=1, source_target_pairs={{0,8},{8,0},{1,9},{9,1},{2,10},{10,2},{3,11},{11,3},{4,12},{12,4},... | collective-permute-start | bytes 1572872 | tf_op jit(solution)/shard_map/ppermute | solution.py:162
  47.6 1.9 %collective-permute-done.other_ref = f32[1024,128]{1,0:T(8,128)S(1)} collective-permute-done((f32[1024,128]{1,0:T(8,128)S(1)}, f32[1024,128]{1,0:T(8,128)S(1)}, u32[]{:S(2)}, u32[]{:S(2)}) %collective-permute-start) | collective-permute-done | bytes 524320 | tf_op jit(solution)/shard_map/ppermute | solution.py:162
  49.5 0.0 copy-done.4
  49.5 0.8 %shard_map.76 = f32[1024,128]{1,0:T(8,128)S(1)} custom-call(s32[2,128]{1,0:T(2,128)S(1)} %bitcast.14, s32[1]{0:T(128)} %bitcast.1.core_ref, f32[1024,128]{1,0:T(8,128)S(1)} %shard_map.75.own_ref, f32[1024,128]{1,0:T(8,128)S(1)} %collective-permute-done.other_ref), custom_call_target="tpu_custom_call" | custom-call | tf_op jit(solution)/shard_map/pallas_call | solution.py:103
  50.3 27.8 %all_to_all.16.terms_ref = f32[64,16,128]{2,1,0:T(8,128)S(1)} all-to-all(f32[64,16,128]{2,1,0:T(8,128)S(1)} %bitcast.12), channel_id=1, replica_groups=mesh['layer'=4,'y'=8,'core'=2,'tile'=8] {'tile','y'}, dimensions={0} | all-to-all | bytes 1048576 | tf_op jit(solution)/shard_map/all_to_all | solution.py:164
  78.1 0.0 copy-done.3
  78.1 1.0 %shard_map.77 = f32[1,256,256]{2,1,0:T(8,128)} custom-call(f32[64,16,128]{2,1,0:T(8,128)S(1)} %all_to_all.16.terms_ref, f32[1,256,256]{2,1,0:T(8,128)S(1)} %copy-done.3), custom_call_target="tpu_custom_call" | custom-call | tf_op jit(solution)/shard_map/pallas_call | solution.py:133
  (4 shorter events, 0.1 us)
Async XLA Ops:
  0.0 1.1 %copy-start = (bf16[4,192,512]{2,1,0:T(8,128)(2,1)S(1)}, bf16[4,192,512]{2,1,0:T(8,128)(2,1)}, u32[]{:S(2)}) copy-start(bf16[4,192,512]{2,1,0:T(8,128)(2,1)} %param.7) | copy-start | bytes 2359300
  0.0 13.6 %copy-start.2 = (bf16[1792,256]{1,0:T(8,128)(2,1)S(1)}, bf16[1792,256]{1,0:T(8,128)(2,1)}, u32[]{:S(2)}) copy-start(bf16[1792,256]{1,0:T(8,128)(2,1)} %w_ref.1) | copy-start | bytes 2752516
  3.1 13.7 %copy-start.5 = (s32[4]{0:T(128)S(1)}, s32[4]{0:T(128)}, u32[]{:S(2)}) copy-start(s32[4]{0:T(128)} %param.11) | copy-start | bytes 52
  3.1 25.1 %all-to-all-start = ((f32[8,96,128]{2,1,0:T(8,128)}), f32[8,96,128]{2,1,0:T(8,128)S(1)}, u32[]{:S(2)}, u32[]{:S(2)}) async-start(f32[8,96,128]{2,1,0:T(8,128)} %fusion), calls=%async_computation | async-start | bytes 786432 | tf_op jit(solution)/shard_map/all_to_all | solution.py:149
  13.6 1.8 %copy-start.1 = (bf16[4,192,1792]{2,1,0:T(8,128)(2,1)S(1)}, bf16[4,192,1792]{2,1,0:T(8,128)(2,1)}, u32[]{:S(2)}) copy-start(bf16[4,192,1792]{2,1,0:T(8,128)(2,1)} %x_ref.1) | copy-start | bytes 8257540
  16.8 32.6 %copy-start.4 = (s32[128,2]{0,1:T(2,128)S(1)}, s32[128,2]{0,1:T(2,128)}, u32[]{:S(2)}) copy-start(s32[128,2]{0,1:T(2,128)} %param.12) | copy-start | bytes 3076
  28.4 49.7 %copy-start.3 = (f32[1,256,256]{2,1,0:T(8,128)S(1)}, f32[1,256,256]{2,1,0:T(8,128)}, u32[]{:S(2)}) copy-start(f32[1,256,256]{2,1,0:T(8,128)} %prior_ref.1) | copy-start | bytes 786436
  45.7 3.8 %collective-permute-start = (f32[1024,128]{1,0:T(8,128)S(1)}, f32[1024,128]{1,0:T(8,128)S(1)}, u32[]{:S(2)}, u32[]{:S(2)}) collective-permute-start(f32[1024,128]{1,0:T(8,128)S(1)} %shard_map.75.own_ref), channel_id=1, source_target_pairs={{0,8},{8,0},{1,9},{9,1},{2,10},{10,2},{3,11},{11,3},{4,12},{12,4},... | collective-permute-start | bytes 1572872 | tf_op jit(solution)/shard_map/ppermute | solution.py:162

commit v4 on v0

v4 whole, which is shorter than its diff:
```python
import functools

import jax
import jax.numpy as jnp
from jax import lax
from jax.experimental import pallas as pl
from jax.experimental.pallas import tpu as pltpu
from jax.sharding import Mesh
from jax.sharding import PartitionSpec as P

PROJECT_VMEM = 60 * 1024 * 1024
VMEM_LIMIT = 4 * 1024 * 1024
ANY = pl.BlockSpec(memory_space=pl.ANY)
VMEM = pl.BlockSpec(memory_space=pltpu.VMEM)
SMEM = pl.BlockSpec(memory_space=pltpu.SMEM)
PARAMS = pltpu.CompilerParams(vmem_limit_bytes=VMEM_LIMIT)


def high_and_rest(x):
    high = x.astype(jnp.bfloat16)
    return high, (x - high.astype(jnp.float32)).astype(jnp.bfloat16)


def project_kernel(
    act_ref, grad_ref, in_ref, out_ref, len_ref, o_ref, weight_ref, act, grad, side_in, side_out, lengths, sems, grad_sems
):
    seqs, tok, _ = act.shape
    width_in = side_in.shape[1]
    rows = weight_ref.shape[0]
    half = seqs // 2
    copy_in = pltpu.make_async_copy(in_ref, side_in, sems.at[0])
    copy_act = pltpu.make_async_copy(act_ref, act, sems.at[1])
    copy_out = pltpu.make_async_copy(out_ref, side_out, sems.at[2])
    copy_len = pltpu.make_async_copy(len_ref, lengths, sems.at[3])
    parts = [pl.ds(part * half, half) for part in range(2)]
    copies = [pltpu.make_async_copy(grad_ref.at[p], grad.at[p], grad_sems.at[n]) for n, p in enumerate(parts)]
    copy_in.start()
    copy_act.start()
    copy_out.start()
    copy_len.start()
    for copy in copies:
        copy.start()
    copy_in.wait()
    copy_act.wait()
    for s in range(seqs):
        o_ref[s * tok:(s + 1) * tok, :width_in] = jnp.dot(
            act[s], side_in[...], preferred_element_type=jnp.float32
        )
    copy_out.wait()
    copy_len.wait()
    first = lax.axis_index("tile") * rows
    length = lengths[first // tok]
    position = (lax.axis_index("y") * 2 + lax.axis_index("core")) * tok + first % tok
    position = position + lax.broadcasted_iota(jnp.int32, weight_ref.shape, 0)
    scale = lax.rsqrt(jnp.full(weight_ref.shape, length, jnp.int32).astype(jnp.float32))
    weight_ref[...] = jnp.where(position < length, scale, 0.0)
    for part in range(2):
        copies[part].wait()
        for s in range(part * half, (part + 1) * half):
            o_ref[s * tok:(s + 1) * tok, width_in:] = jnp.dot(
                grad[s], side_out[...], preferred_element_type=jnp.float32
            )


def project(activations, out_grads, proj_in, proj_out, seq_lengths, rows):
    seqs, tok, dim = activations.shape
    hidden = out_grads.shape[2]
    width_in, width_out = proj_in.shape[1], proj_out.shape[1]
    width = width_in + width_out
    return pl.pallas_call(
        project_kernel,
        out_shape=(
            jax.ShapeDtypeStruct((seqs * tok, width), jnp.float32),
            jax.ShapeDtypeStruct((rows, width_in), jnp.float32),
        ),
        in_specs=[ANY] * 5,
        out_specs=(VMEM, VMEM),
        scratch_shapes=[
            pltpu.VMEM(activations.shape, activations.dtype),
            pltpu.VMEM(out_grads.shape, out_grads.dtype),
            pltpu.VMEM(proj_in.shape, proj_in.dtype),
            pltpu.VMEM(proj_out.shape, proj_out.dtype),
            pltpu.SMEM(seq_lengths.shape, seq_lengths.dtype),
            pltpu.SemaphoreType.DMA((4,)),
            pltpu.SemaphoreType.DMA((2,)),
        ],
        compiler_params=pltpu.CompilerParams(vmem_limit_bytes=PROJECT_VMEM),
        cost_estimate=pl.CostEstimate(
            flops=2 * seqs * tok * (dim * width_in + hidden * width_out),
            bytes_accessed=2 * seqs * tok * (dim + hidden) + 4 * seqs * tok * width,
            transcendentals=0,
        ),
    )(activations, out_grads, proj_in, proj_out, seq_lengths)


def combine_kernel(terms_ref, weight_ref, o_ref):
    width_in = weight_ref.shape[1]
    o_ref[:, :width_in] = jnp.sum(terms_ref[:, :, :width_in], axis=0) * weight_ref[...]
    o_ref[:, width_in:] = jnp.sum(terms_ref[:, :, width_in:], axis=0)


def combine(terms, weight):
    return pl.pallas_call(
        combine_kernel,
        out_shape=jax.ShapeDtypeStruct(terms.shape[1:], jnp.float32),
        in_specs=[VMEM] * 2,
        out_specs=VMEM,
        compiler_params=PARAMS,
    )(terms, weight)


def expand_kernel(chips, map_ref, own_ref, other_ref, o_ref, product_ref, blocks_ref):
    width_in = o_ref.shape[1]
    lefts, rights = [], []
    for ref in (own_ref, other_ref):
        left_high, left_rest = high_and_rest(ref[:, :width_in])
        right_high, right_rest = high_and_rest(ref[:, width_in:])
        lefts += [left_high, left_rest, left_high]
        rights += [right_high, right_high, right_rest]
    product_ref[...] = lax.dot_general(
        jnp.concatenate(rights, axis=0),
        jnp.concatenate(lefts, axis=0),
        (((0,), (0,)), ((), ())),
        preferred_element_type=jnp.float32,
    )
    count = product_ref.shape[0] // 2
    for r in range(2):
        rows = product_ref[pl.ds(r, count, stride=2), :]
        for again in range(4):
            blocks_ref[pl.ds(2 * again + r, count, stride=8), :] = rows
    core = lax.axis_index("core")
    owners = o_ref.shape[0] // 4
    pieces = owners // chips
    row = lax.broadcasted_iota(jnp.int32, (8, width_in), 0)
    for n in range(0, owners, 2):
        sides = []
        for owner in (n, n + 1):
            k = (2 * (owner % chips) + core) * pieces + owner // chips
            for side in range(2):
                sides.append(blocks_ref[pl.ds(pl.multiple_of(map_ref[side, k] * 8, 8), 8), :])
        low = jnp.where(row < 2, sides[0], sides[1])
        high = jnp.where(row < 6, sides[2], sides[3])
        o_ref[4 * n:4 * n + 8, :] = jnp.where(row < 4, low, high)


def expand(tile_map, own, other, width_in, owners, chips):
    width_out = own.shape[1] - width_in
    return pl.pallas_call(
        functools.partial(expand_kernel, chips),
        out_shape=jax.ShapeDtypeStruct((owners * 4, width_in), jnp.float32),
        in_specs=[SMEM, VMEM, VMEM],
        out_specs=VMEM,
        scratch_shapes=[
            pltpu.VMEM((width_out, width_in), jnp.float32),
            pltpu.VMEM((4 * width_out, width_in), jnp.float32),
        ],
        compiler_params=PARAMS,
    )(tile_map.T, own, other)


def covariance_kernel(terms_ref, prior_ref, o_ref):
    blocks = jnp.sum(terms_ref[...], axis=1)
    blocks = blocks[:, 0:4] + blocks[:, 4:8]
    left = jnp.concatenate([blocks[:, 0], blocks[:, 1]], axis=1)
    right = jnp.concatenate([blocks[:, 2], blocks[:, 3]], axis=1)
    left_high, left_rest = high_and_rest(left)
    right_high, right_rest = high_and_rest(right)
    product = lax.dot_general(
        jnp.concatenate([left_high, left_high, left_rest], axis=0),
        jnp.concatenate([right_high, right_rest, right_high], axis=0),
        (((0,), (0,)), ((), ())),
        preferred_element_type=jnp.float32,
    )
    o_ref[0] = prior_ref[0] + product


def covariance(terms, prior_cov):
    return pl.pallas_call(
        covariance_kernel,
        out_shape=jax.ShapeDtypeStruct(prior_cov.shape, jnp.float32),
        in_specs=[VMEM] * 2,
        out_specs=VMEM,
        compiler_params=PARAMS,
    )(terms, prior_cov)


def body(activations, out_grads, proj_in, proj_out, seq_lengths, tile_map, prior_cov):
    seqs, tok, _ = activations.shape
    width_in = proj_in.shape[1]
    pieces, chips = lax.axis_size("tile"), lax.axis_size("y")
    rows = seqs * tok // pieces
    owners = chips * pieces
    partial, weight = project(activations, out_grads, proj_in, proj_out, seq_lengths, rows)
    arrived = lax.all_to_all(partial.reshape(pieces, rows, -1), "tile", 0, 0, tiled=True)
    own = combine(arrived, weight)
    other = lax.ppermute(own, "core", [(0, 1), (1, 0)])
    terms = expand(tile_map, own, other, width_in, owners, chips)
    terms = lax.all_to_all(terms.reshape(owners, 4, width_in), ("tile", "y"), 0, 0, tiled=True)
    return covariance(terms.reshape(seqs, owners // (2 * seqs), 8, width_in), prior_cov)


def solution(mesh):
    layers, seq, tile = (mesh.shape[name] for name in ("layer", "seq", "tile"))
    fine = Mesh(mesh.devices.reshape(layers, seq // 2, 2, tile), ("layer", "y", "core", "tile"))
    tokens = P("layer", ("y", "core"), "tile")
    features = P(("layer", "tile"), None)
    tiles = P(("layer", "y", "core", "tile"), None, None)
    return jax.shard_map(
        body,
        mesh=fine,
        in_specs=(tokens, tokens, features, features, P(), P(), tiles),
        out_specs=tiles,
        check_vma=False,
    )
```

time: 484 us -> 72.6 us (0.15)
  waiting for transfers between devices: 308 us -> 1.34 us
  blocking collectives: 137 us -> 62.8 us
  local copies, waits for them, and re-layouts: 18.5 us -> 0.01 us
  between operations: 13.5 us -> 0.04 us
  Pallas kernels: 0 us -> 6.13 us
  matrix products: 5.56 us -> 0 us
    reduce_scatter x1 -> x0, waiting for transfers between devices: 221 us -> none  [body(): lax.psum_scatter(partial_value, ('seq', 'tile'), scatter_dimension=1, til...]
    all_gather x1 -> x0, blocking collectives: 137 us -> none  [body(): shard_piece = lax.all_gather(features, ('seq', 'tile'), axis=1, tiled=True)]
    psum x1 -> x0, waiting for transfers between devices: 86.7 us -> none  [body(): totals = lax.psum(whole_term, 'tile')]
    all_to_all x0 -> x2, blocking collectives: none -> 62.8 us  [the longest x1 42 us: body(): lax.all_to_all(partial.reshape(pieces, rows, -1), 'tile', 0, 0, tiled=True)]
    reshape x1 -> x0, local copies, waits for them, and re-layouts: 8.7 us -> none  [body(): partial_value = partial_value.reshape(seq_count, width_out * width_in)]
    gather x1 -> x0, local copies, waits for them, and re-layouts: 6.8 us -> none  [body(): jnp.take(shard_piece, jnp.clip(columns, 0, piece_width - 1), axis=1)]
    pallas_call x0 -> x4, Pallas kernels: none -> 6.13 us  [the longest x1 4.05 us: project(): pl.pallas_call(project_kernel, out_shape=(jax.ShapeDtypeStruct((seqs * to...]
    dot_general x4 -> x0, matrix products: 5.56 us -> none  [the longest x1 2.1 us: project_tokens(): jnp.einsum('slc,ck->lsk', grad_rows, proj_out, preferred_element_type=jnp...]
  transfers between devices with their start and end apart: 2 -> 1, of which waited for: 2 -> 1; matrix products, arithmetic and copies ran while one was open for 0% -> 0% of each run, Pallas kernels for 0% -> 0%
where the time goes in v4:
time: 72.6 us; the launch traced here: 72.4 us
  blocking collectives  62.8 us (87%)
  Pallas kernels  6.13 us (8%)
  starting transfers between devices  2.05 us (3%)
  waiting for transfers between devices  1.34 us (2%)
    all_to_all x1, blocking collectives, body(): lax.all_to_all(partial.reshape(pieces, rows, -1), 'tile', 0, 0, tiled=True)  42 us
    all_to_all x1, blocking collectives, body(): lax.all_to_all(terms.reshape(owners, 4, width_in), ('tile', 'y'), 0, 0, t...  20.8 us
    pallas_call x1, Pallas kernels, project(): pl.pallas_call(project_kernel, out_shape=(jax.ShapeDtypeStruct((seqs * to...  4.05 us
    ppermute x1, starting transfers between devices, body(): other = lax.ppermute(own, 'core', [(0, 1), (1, 0)])  2.05 us
  transfers between devices with their start and end apart: 1, of which 1 were waited for; matrix products, arithmetic and copies ran while one was open for 0% of the time, Pallas kernels for 0%

profile of v4, /device:TPU:6, one launch (start us, length us, event | category | flops | bytes accessed | tf_op | source)
XLA Modules:
  0.0 72.4 jit_solution(12574486452432437565)
XLA Ops:
  0.0 4.1 %shard_map.73 = (f32[768,384]{1,0:T(8,128)}, f32[96,128]{1,0:T(8,128)}) custom-call(bf16[4,192,512]{2,1,0:T(8,128)(2,1)} %act_ref.1, bf16[4,192,1792]{2,1,0:T(8,128)(2,1)} %grad_ref.1, bf16[512,128]{1,0:T(8,128)(2,1)} %in_ref.1, bf16[1792,256]{1,0:T(8,128)(2,1)} %out_ref.1, s32[4]{0:T(128)} %len_ref.1), custom_call_target="tpu_custom_call" | custom-call | flops 805306368 | bytes 4718592 | tf_op jit(solution)/shard_map/pallas_call | solution.py:70
  4.1 0.0 copy-start.1
  4.1 42.0 %all_to_all.10.terms_ref = f32[8,96,384]{2,1,0:T(8,128)S(1)} all-to-all(f32[8,96,384]{2,1,0:T(8,128)} %bitcast.7), channel_id=1, replica_groups=mesh['layer'=4,'y'=8,'core'=2,'tile'=8] {'tile'}, dimensions={0} | all-to-all | bytes 2359296 | tf_op jit(solution)/shard_map/all_to_all | solution.py:194
  46.1 0.0 copy-start.2
  46.1 0.0 copy-start
  46.1 0.0 copy-done.1
  46.1 0.1 shard_map.74.own_ref
  46.1 2.1 %collective-permute-start = (f32[96,384]{1,0:T(8,128)S(1)}, f32[96,384]{1,0:T(8,128)S(1)}, u32[]{:S(2)}, u32[]{:S(2)}) collective-permute-start(f32[96,384]{1,0:T(8,128)S(1)} %shard_map.74.own_ref), channel_id=1, source_target_pairs={{0,8},{8,0},{1,9},{9,1},{2,10},{10,2},{3,11},{11,3},{4,12},{12,4},... | collective-permute-start | bytes 442376 | tf_op jit(solution)/shard_map/ppermute | solution.py:196
  48.2 1.3 %collective-permute-done.other_ref = f32[96,384]{1,0:T(8,128)S(1)} collective-permute-done((f32[96,384]{1,0:T(8,128)S(1)}, f32[96,384]{1,0:T(8,128)S(1)}, u32[]{:S(2)}, u32[]{:S(2)}) %collective-permute-start) | collective-permute-done | bytes 147488 | tf_op jit(solution)/shard_map/ppermute | solution.py:196
  49.5 0.0 copy-done.2
  49.5 1.1 %shard_map.75 = f32[256,128]{1,0:T(8,128)S(1)} custom-call(s32[2,128]{1,0:T(2,128)S(1)} %bitcast.6, f32[96,384]{1,0:T(8,128)S(1)} %shard_map.74.own_ref, f32[96,384]{1,0:T(8,128)S(1)} %collective-permute-done.other_ref), custom_call_target="tpu_custom_call" | custom-call | tf_op jit(solution)/shard_map/pallas_call | solution.py:148
  50.6 20.8 %all_to_all.11 = f32[64,4,128]{2,1,0:T(4,128)S(1)} all-to-all(f32[64,4,128]{2,1,0:T(4,128)S(1)} %bitcast.5), channel_id=1, replica_groups=mesh['layer'=4,'y'=8,'core'=2,'tile'=8] {'tile','y'}, dimensions={0} | all-to-all | bytes 262144 | tf_op jit(solution)/shard_map/all_to_all | solution.py:198
  71.4 0.0 copy-done
  71.4 0.9 %shard_map.76 = f32[1,256,256]{2,1,0:T(8,128)} custom-call(f32[4,8,8,128]{3,2,1,0:T(8,128)S(1)} %bitcast.4, f32[1,256,256]{2,1,0:T(8,128)S(1)} %copy-done), custom_call_target="tpu_custom_call" | custom-call | tf_op jit(solution)/shard_map/pallas_call | solution.py:178
Async XLA Ops:
  4.1 42.0 %copy-start.1 = (f32[96,128]{1,0:T(8,128)S(1)}, f32[96,128]{1,0:T(8,128)}, u32[]{:S(2)}) copy-start(f32[96,128]{1,0:T(8,128)} %get-tuple-element.8.weight_ref) | copy-start | bytes 147460
  46.1 3.5 %copy-start.2 = (s32[128,2]{0,1:T(2,128)S(1)}, s32[128,2]{0,1:T(2,128)}, u32[]{:S(2)}) copy-start(s32[128,2]{0,1:T(2,128)} %param.12) | copy-start | bytes 3076
  46.1 25.3 %copy-start = (f32[1,256,256]{2,1,0:T(8,128)S(1)}, f32[1,256,256]{2,1,0:T(8,128)}, u32[]{:S(2)}) copy-start(f32[1,256,256]{2,1,0:T(8,128)} %prior_ref.1) | copy-start | bytes 786436
  46.1 3.4 %collective-permute-start = (f32[96,384]{1,0:T(8,128)S(1)}, f32[96,384]{1,0:T(8,128)S(1)}, u32[]{:S(2)}, u32[]{:S(2)}) collective-permute-start(f32[96,384]{1,0:T(8,128)S(1)} %shard_map.74.own_ref), channel_id=1, source_target_pairs={{0,8},{8,0},{1,9},{9,1},{2,10},{10,2},{3,11},{11,3},{4,12},{12,4},... | collective-permute-start | bytes 442376 | tf_op jit(solution)/shard_map/ppermute | solution.py:196

commit v5 on v4

--- a/solution.py
+++ b/solution.py
@@ -22,44 +22,59 @@
 
 
 def project_kernel(
-    act_ref, grad_ref, in_ref, out_ref, len_ref, o_ref, weight_ref, act, grad, side_in, side_out, lengths, sems, grad_sems
+    act_ref, grad_ref, in_ref, out_ref, len_ref, keep_ref, up_ref, down_ref,
+    act, grad, side_in, side_out, lengths, held, sems, grad_sems, held_sems
 ):
     seqs, tok, _ = act.shape
     width_in = side_in.shape[1]
-    rows = weight_ref.shape[0]
+    rows = held.shape[1]
     half = seqs // 2
+    pieces = held.shape[0]
+
+    def store(s, columns, value):
+        for part in range(tok // rows):
+            ahead = lax.rem(s * (tok // rows) + part - lax.axis_index("tile") + pieces, pieces)
+            slot = jnp.int32(0)
+            for place, distance in enumerate((0, 1, 7, 4, 2, 5, 6, 3)):
+                slot = jnp.where(ahead == distance, place, slot)
+            held[slot, :, columns] = value[part * rows:(part + 1) * rows]
+
     copy_in = pltpu.make_async_copy(in_ref, side_in, sems.at[0])
     copy_act = pltpu.make_async_copy(act_ref, act, sems.at[1])
     copy_out = pltpu.make_async_copy(out_ref, side_out, sems.at[2])
     copy_len = pltpu.make_async_copy(len_ref, lengths, sems.at[3])
     parts = [pl.ds(part * half, half) for part in range(2)]
     copies = [pltpu.make_async_copy(grad_ref.at[p], grad.at[p], grad_sems.at[n]) for n, p in enumerate(parts)]
+    copy_len.start()
     copy_in.start()
     copy_act.start()
     copy_out.start()
-    copy_len.start()
     for copy in copies:
         copy.start()
+    position = lax.broadcasted_iota(jnp.int32, (tok, width_in), 0)
+    position = position + (lax.axis_index("y") * 2 + lax.axis_index("core")) * tok
     copy_in.wait()
+    copy_len.wait()
     copy_act.wait()
     for s in range(seqs):
-        o_ref[s * tok:(s + 1) * tok, :width_in] = jnp.dot(
-            act[s], side_in[...], preferred_element_type=jnp.float32
-        )
+        left = jnp.dot(act[s], side_in[...], preferred_element_type=jnp.float32)
+        scale = lax.rsqrt(jnp.full(position.shape, lengths[s], jnp.int32).astype(jnp.float32))
+        store(s, slice(0, width_in), left * jnp.where(position < lengths[s], scale, 0.0))
     copy_out.wait()
-    copy_len.wait()
-    first = lax.axis_index("tile") * rows
-    length = lengths[first // tok]
-    position = (lax.axis_index("y") * 2 + lax.axis_index("core")) * tok + first % tok
-    position = position + lax.broadcasted_iota(jnp.int32, weight_ref.shape, 0)
-    scale = lax.rsqrt(jnp.full(weight_ref.shape, length, jnp.int32).astype(jnp.float32))
-    weight_ref[...] = jnp.where(position < length, scale, 0.0)
     for part in range(2):
         copies[part].wait()
         for s in range(part * half, (part + 1) * half):
-            o_ref[s * tok:(s + 1) * tok, width_in:] = jnp.dot(
-                grad[s], side_out[...], preferred_element_type=jnp.float32
-            )
+            right = jnp.dot(grad[s], side_out[...], preferred_element_type=jnp.float32)
+            store(s, slice(width_in, None), right)
+    leave = [
+        pltpu.make_async_copy(held.at[pl.ds(4, 2)], up_ref, held_sems.at[0]),
+        pltpu.make_async_copy(held.at[pl.ds(6, 2)], down_ref, held_sems.at[1]),
+        pltpu.make_async_copy(held.at[pl.ds(0, 4)], keep_ref, held_sems.at[2]),
+    ]
+    for copy in leave:
+        copy.start()
+    for copy in leave:
+        copy.wait()
 
 
 def project(activations, out_grads, proj_in, proj_out, seq_lengths, rows):
@@ -70,19 +85,22 @@
     return pl.pallas_call(
         project_kernel,
         out_shape=(
-            jax.ShapeDtypeStruct((seqs * tok, width), jnp.float32),
-            jax.ShapeDtypeStruct((rows, width_in), jnp.float32),
+            jax.ShapeDtypeStruct((4, rows, width), jnp.float32),
+            jax.ShapeDtypeStruct((2, rows, width), jnp.float32),
+            jax.ShapeDtypeStruct((2, rows, width), jnp.float32),
         ),
         in_specs=[ANY] * 5,
-        out_specs=(VMEM, VMEM),
+        out_specs=(ANY,) * 3,
         scratch_shapes=[
             pltpu.VMEM(activations.shape, activations.dtype),
             pltpu.VMEM(out_grads.shape, out_grads.dtype),
             pltpu.VMEM(proj_in.shape, proj_in.dtype),
             pltpu.VMEM(proj_out.shape, proj_out.dtype),
             pltpu.SMEM(seq_lengths.shape, seq_lengths.dtype),
+            pltpu.VMEM((8, rows, width), jnp.float32),
             pltpu.SemaphoreType.DMA((4,)),
             pltpu.SemaphoreType.DMA((2,)),
+            pltpu.SemaphoreType.DMA((3,)),
         ],
         compiler_params=pltpu.CompilerParams(vmem_limit_bytes=PROJECT_VMEM),
         cost_estimate=pl.CostEstimate(
@@ -93,20 +111,66 @@
     )(activations, out_grads, proj_in, proj_out, seq_lengths)
 
 
-def combine_kernel(terms_ref, weight_ref, o_ref):
-    width_in = weight_ref.shape[1]
-    o_ref[:, :width_in] = jnp.sum(terms_ref[:, :, :width_in], axis=0) * weight_ref[...]
-    o_ref[:, width_in:] = jnp.sum(terms_ref[:, :, width_in:], axis=0)
-
-
-def combine(terms, weight):
-    return pl.pallas_call(
-        combine_kernel,
-        out_shape=jax.ShapeDtypeStruct(terms.shape[1:], jnp.float32),
-        in_specs=[VMEM] * 2,
-        out_specs=VMEM,
-        compiler_params=PARAMS,
-    )(terms, weight)
+def hold_kernel(keep_ref, held_ref):
+    pass
+
+
+def hold(keep):
+    return pl.pallas_call(
+        hold_kernel,
+        out_shape=jax.ShapeDtypeStruct(keep.shape, keep.dtype),
+        in_specs=[VMEM],
+        out_specs=VMEM,
+        input_output_aliases={0: 0},
+        compiler_params=PARAMS,
+    )(keep)
+
+
+def far_kernel(keep_ref, below_ref, above_ref, far_ref):
+    far_ref[...] = keep_ref[3] + below_ref[1] + above_ref[1]
+
+
+def near_kernel(keep_ref, below_ref, above_ref, far_ref, plus_ref, minus_ref):
+    plus_ref[...] = keep_ref[1] + below_ref[0]
+    minus_ref[...] = keep_ref[2] + above_ref[0]
+
+
+def gather_far(keep, below, above):
+    return pl.pallas_call(
+        far_kernel,
+        out_shape=jax.ShapeDtypeStruct(keep.shape[1:], jnp.float32),
+        in_specs=[VMEM] * 3,
+        out_specs=VMEM,
+        compiler_params=PARAMS,
+    )(keep, below, above)
+
+
+def gather_near(keep, below, above, far):
+    return pl.pallas_call(
+        near_kernel,
+        out_shape=(jax.ShapeDtypeStruct(keep.shape[1:], jnp.float32),) * 2,
+        in_specs=[VMEM] * 4,
+        out_specs=(VMEM,) * 2,
+        compiler_params=PARAMS,
+    )(keep, below, above, far)
+
+
+def first_kernel(keep_ref, far_ref, o_ref):
+    o_ref[...] = keep_ref[0] + far_ref[...]
+
+
+def last_kernel(first_ref, plus_ref, minus_ref, o_ref):
+    o_ref[...] = first_ref[...] + plus_ref[...] + minus_ref[...]
+
+
+def combine(keep, far, plus, minus):
+    piece = jax.ShapeDtypeStruct(plus.shape, jnp.float32)
+    first = pl.pallas_call(
+        first_kernel, out_shape=piece, in_specs=[VMEM] * 2, out_specs=VMEM, compiler_params=PARAMS
+    )(keep, far)
+    return pl.pallas_call(
+        last_kernel, out_shape=piece, in_specs=[VMEM] * 3, out_specs=VMEM, compiler_params=PARAMS
+    )(first, plus, minus)
 
 
 def expand_kernel(chips, map_ref, own_ref, other_ref, o_ref, product_ref, blocks_ref):
@@ -190,9 +254,17 @@
     pieces, chips = lax.axis_size("tile"), lax.axis_size("y")
     rows = seqs * tok // pieces
     owners = chips * pieces
-    partial, weight = project(activations, out_grads, proj_in, proj_out, seq_lengths, rows)
-    arrived = lax.all_to_all(partial.reshape(pieces, rows, -1), "tile", 0, 0, tiled=True)
-    own = combine(arrived, weight)
+    keep, up, down = project(activations, out_grads, proj_in, proj_out, seq_lengths, rows)
+
+    def shift(x, by):
+        return lax.ppermute(x, "tile", [(i, (i + by) % pieces) for i in range(pieces)])
+
+    below, above = shift(up, 1), shift(down, -1)
+    keep = hold(keep)
+    far = gather_far(keep, below, above)
+    plus, minus = gather_near(keep, below, above, far)
+    far, plus, minus = shift(far, pieces // 2), shift(plus, 1), shift(minus, -1)
+    own = combine(keep, far, plus, minus)
     other = lax.ppermute(own, "core", [(0, 1), (1, 0)])
     terms = expand(tile_map, own, other, width_in, owners, chips)
     terms = lax.all_to_all(terms.reshape(owners, 4, width_in), ("tile", "y"), 0, 0, tiled=True)

time: 72.6 us -> 69.6 us (0.959)
  blocking collectives: 62.8 us -> 23.9 us
  starting transfers between devices: 2.05 us -> 27.3 us
  waiting for transfers between devices: 1.34 us -> 10.6 us
  local copies, waits for them, and re-layouts: 0.01 us -> 1.07 us
    all_to_all x1 -> x0, blocking collectives: 42 us -> none  [body(): lax.all_to_all(partial.reshape(pieces, rows, -1), 'tile', 0, 0, tiled=True)]
    ppermute x0 -> x5, starting transfers between devices: none -> 25.4 us  [shift(): lax.ppermute(x, 'tile', [(i, (i + by) % pieces) for i in range(pieces)])]
    ppermute x0 -> x5, waiting for transfers between devices: none -> 9.22 us  [shift(): lax.ppermute(x, 'tile', [(i, (i + by) % pieces) for i in range(pieces)])]
    all_to_all x1, blocking collectives: 20.8 us -> 23.9 us  [body(): lax.all_to_all(terms.reshape(owners, 4, width_in), ('tile', 'y'), 0, 0, t...]
    unnamed x6, local copies, waits for them, and re-layouts: 0.01 us -> 1.07 us
    pallas_call x2 -> x6, Pallas kernels: 4.11 us -> 4.2 us  [the longest x1 4.1 us: project(): pl.pallas_call(project_kernel, out_shape=(jax.ShapeDtypeStruct((4, rows,...]
  transfers between devices with their start and end apart: 1 -> 6, of which waited for: 1 -> 6; matrix products, arithmetic and copies ran while one was open for 0% -> 0% of each run, Pallas kernels for 0% -> 0%
where the time goes in v5:
time: 69.6 us; the launch traced here: 69.2 us
  starting transfers between devices  27.3 us (39%)
  blocking collectives  23.9 us (34%)
  waiting for transfers between devices  10.6 us (15%)
  Pallas kernels  6.22 us (9%)
  local copies, waits for them, and re-layouts  1.07 us (2%)
    ppermute x5, starting transfers between devices, shift(): lax.ppermute(x, 'tile', [(i, (i + by) % pieces) for i in range(pieces)])  25.4 us
    all_to_all x1, blocking collectives, body(): lax.all_to_all(terms.reshape(owners, 4, width_in), ('tile', 'y'), 0, 0, t...  23.9 us
    ppermute x5, waiting for transfers between devices, shift(): lax.ppermute(x, 'tile', [(i, (i + by) % pieces) for i in range(pieces)])  9.22 us
    pallas_call x1, Pallas kernels, project(): pl.pallas_call(project_kernel, out_shape=(jax.ShapeDtypeStruct((4, rows,...  4.1 us
    ppermute x1, starting transfers between devices, body(): other = lax.ppermute(own, 'core', [(0, 1), (1, 0)])  1.92 us
  transfers between devices with their start and end apart: 6, of which 6 were waited for; matrix products, arithmetic and copies ran while one was open for 0% of the time, Pallas kernels for 0%

profile of v5, /device:TPU:6, one launch (start us, length us, event | category | flops | bytes accessed | tf_op | source)
XLA Modules:
  0.0 69.2 jit_solution(9645361020086873671)
XLA Ops:
  0.0 4.1 %shard_map.73 = (f32[4,96,384]{2,1,0:T(8,128)}, f32[2,96,384]{2,1,0:T(8,128)}, f32[2,96,384]{2,1,0:T(8,128)}) custom-call(bf16[4,192,512]{2,1,0:T(8,128)(2,1)} %act_ref.1, bf16[4,192,1792]{2,1,0:T(8,128)(2,1)} %grad_ref.1, bf16[512,128]{1,0:T(8,128)(2,1)} %in_ref.1, bf16[1792,256]{1,0:T(8,128)(2,1)} %out_ref.1, s32[4]{0:T(128)} %len_ref.1), custom_call_target="tpu_custom_call" | custom-call | flops 805306368 | bytes 4718592 | tf_op jit(solution)/shard_map/pallas_call | solution.py:85
  4.1 0.0 copy-start.2
  4.1 4.3 %collective-permute-start = (f32[2,96,384]{2,1,0:T(8,128)}, f32[2,96,384]{2,1,0:T(8,128)S(1)}, u32[]{:S(2)}, u32[]{:S(2)}) collective-permute-start(f32[2,96,384]{2,1,0:T(8,128)} %get-tuple-element.11), channel_id=1, source_target_pairs={{0,1},{1,2},{2,3},{3,4},{4,5},{5,6},{6,7},{7,0},{8,9},{9,10},{10,1... | collective-permute-start | bytes 884744 | tf_op jit(solution)/shard_map/ppermute | solution.py:260
  8.4 8.6 %collective-permute-start.1 = (f32[2,96,384]{2,1,0:T(8,128)}, f32[2,96,384]{2,1,0:T(8,128)S(1)}, u32[]{:S(2)}, u32[]{:S(2)}) collective-permute-start(f32[2,96,384]{2,1,0:T(8,128)} %get-tuple-element.12), channel_id=1, source_target_pairs={{0,7},{1,0},{2,1},{3,2},{4,3},{5,4},{6,5},{7,6},{8,15},{9,8},{10,9... | collective-permute-start | bytes 884744 | tf_op jit(solution)/shard_map/ppermute | solution.py:260
  17.0 0.0 copy-start
  17.0 1.1 %copy-done = f32[4,96,384]{2,1,0:T(8,128)S(1)} copy-done((f32[4,96,384]{2,1,0:T(8,128)S(1)}, f32[4,96,384]{2,1,0:T(8,128)}, u32[]{:S(2)}) %copy-start) | copy-done | bytes 589848
  18.1 0.0 copy-start.1
  18.1 4.2 %collective-permute-done.below_ref = f32[2,96,384]{2,1,0:T(8,128)S(1)} collective-permute-done((f32[2,96,384]{2,1,0:T(8,128)}, f32[2,96,384]{2,1,0:T(8,128)S(1)}, u32[]{:S(2)}, u32[]{:S(2)}) %collective-permute-start) | collective-permute-done | bytes 294944 | tf_op jit(solution)/shard_map/ppermute | solution.py:260
  22.3 1.3 %collective-permute-done.1.above_ref = f32[2,96,384]{2,1,0:T(8,128)S(1)} collective-permute-done((f32[2,96,384]{2,1,0:T(8,128)}, f32[2,96,384]{2,1,0:T(8,128)S(1)}, u32[]{:S(2)}, u32[]{:S(2)}) %collective-permute-start.1) | collective-permute-done | bytes 294944 | tf_op jit(solution)/shard_map/ppermute | solution.py:260
  23.6 5.4 %collective-permute-start.2 = (f32[96,384]{1,0:T(8,128)S(1)}, f32[96,384]{1,0:T(8,128)S(1)}, u32[]{:S(2)}, u32[]{:S(2)}) collective-permute-start(f32[96,384]{1,0:T(8,128)S(1)} %shard_map.75.far_ref), channel_id=1, source_target_pairs={{0,4},{1,5},{2,6},{3,7},{4,0},{5,1},{6,2},{7,3},{8,12},{9,13},{10,... | collective-permute-start | bytes 442376 | tf_op jit(solution)/shard_map/ppermute | solution.py:260
  29.1 3.4 %collective-permute-start.3 = (f32[96,384]{1,0:T(8,128)S(1)}, f32[96,384]{1,0:T(8,128)S(1)}, u32[]{:S(2)}, u32[]{:S(2)}) collective-permute-start(f32[96,384]{1,0:T(8,128)S(1)} %get-tuple-element.13), channel_id=1, source_target_pairs={{0,1},{1,2},{2,3},{3,4},{4,5},{5,6},{6,7},{7,0},{8,9},{9,10},{10,1... | collective-permute-start | bytes 442376 | tf_op jit(solution)/shard_map/ppermute | solution.py:260
  32.5 3.7 %collective-permute-start.4 = (f32[96,384]{1,0:T(8,128)S(1)}, f32[96,384]{1,0:T(8,128)S(1)}, u32[]{:S(2)}, u32[]{:S(2)}) collective-permute-start(f32[96,384]{1,0:T(8,128)S(1)} %get-tuple-element.14), channel_id=1, source_target_pairs={{0,7},{1,0},{2,1},{3,2},{4,3},{5,4},{6,5},{7,6},{8,15},{9,8},{10,9... | collective-permute-start | bytes 442376 | tf_op jit(solution)/shard_map/ppermute | solution.py:260
  36.2 1.2 %collective-permute-done.2.far_ref = f32[96,384]{1,0:T(8,128)S(1)} collective-permute-done((f32[96,384]{1,0:T(8,128)S(1)}, f32[96,384]{1,0:T(8,128)S(1)}, u32[]{:S(2)}, u32[]{:S(2)}) %collective-permute-start.2) | collective-permute-done | bytes 147488 | tf_op jit(solution)/shard_map/ppermute | solution.py:260
  37.4 2.2 %collective-permute-done.3.plus_ref = f32[96,384]{1,0:T(8,128)S(1)} collective-permute-done((f32[96,384]{1,0:T(8,128)S(1)}, f32[96,384]{1,0:T(8,128)S(1)}, u32[]{:S(2)}, u32[]{:S(2)}) %collective-permute-start.3) | collective-permute-done | bytes 147488 | tf_op jit(solution)/shard_map/ppermute | solution.py:260
  39.5 0.4 collective-permute-done.4.minus_ref
  39.9 1.9 %collective-permute-start.5 = (f32[96,384]{1,0:T(8,128)S(1)}, f32[96,384]{1,0:T(8,128)S(1)}, u32[]{:S(2)}, u32[]{:S(2)}) collective-permute-start(f32[96,384]{1,0:T(8,128)S(1)} %shard_map.78.own_ref), channel_id=1, source_target_pairs={{0,8},{8,0},{1,9},{9,1},{2,10},{10,2},{3,11},{11,3},{4,12},{12,4},... | collective-permute-start | bytes 442376 | tf_op jit(solution)/shard_map/ppermute | solution.py:268
  41.9 1.3 %collective-permute-done.5.other_ref = f32[96,384]{1,0:T(8,128)S(1)} collective-permute-done((f32[96,384]{1,0:T(8,128)S(1)}, f32[96,384]{1,0:T(8,128)S(1)}, u32[]{:S(2)}, u32[]{:S(2)}) %collective-permute-start.5) | collective-permute-done | bytes 147488 | tf_op jit(solution)/shard_map/ppermute | solution.py:268
  43.2 0.0 copy-done.2
  43.2 1.1 %shard_map.79 = f32[256,128]{1,0:T(8,128)S(1)} custom-call(s32[2,128]{1,0:T(2,128)S(1)} %bitcast.5, f32[96,384]{1,0:T(8,128)S(1)} %shard_map.78.own_ref, f32[96,384]{1,0:T(8,128)S(1)} %collective-permute-done.5.other_ref), custom_call_target="tpu_custom_call" | custom-call | tf_op jit(solution)/shard_map/pallas_call | solution.py:212
  44.3 23.9 %all_to_all.5 = f32[64,4,128]{2,1,0:T(4,128)S(1)} all-to-all(f32[64,4,128]{2,1,0:T(4,128)S(1)} %bitcast.4), channel_id=1, replica_groups=mesh['layer'=4,'y'=8,'core'=2,'tile'=8] {'tile','y'}, dimensions={0} | all-to-all | bytes 262144 | tf_op jit(solution)/shard_map/all_to_all | solution.py:270
  68.2 0.0 copy-done.1
  68.2 0.9 %shard_map.80 = f32[1,256,256]{2,1,0:T(8,128)} custom-call(f32[4,8,8,128]{3,2,1,0:T(8,128)S(1)} %bitcast.3, f32[1,256,256]{2,1,0:T(8,128)S(1)} %copy-done.1), custom_call_target="tpu_custom_call" | custom-call | tf_op jit(solution)/shard_map/pallas_call | solution.py:242
  (5 shorter events, 0.1 us)
Async XLA Ops:
  4.1 39.1 %copy-start.2 = (s32[128,2]{0,1:T(2,128)S(1)}, s32[128,2]{0,1:T(2,128)}, u32[]{:S(2)}) copy-start(s32[128,2]{0,1:T(2,128)} %param.12) | copy-start | bytes 3076
  4.1 18.2 %collective-permute-start = (f32[2,96,384]{2,1,0:T(8,128)}, f32[2,96,384]{2,1,0:T(8,128)S(1)}, u32[]{:S(2)}, u32[]{:S(2)}) collective-permute-start(f32[2,96,384]{2,1,0:T(8,128)} %get-tuple-element.11), channel_id=1, source_target_pairs={{0,1},{1,2},{2,3},{3,4},{4,5},{5,6},{6,7},{7,0},{8,9},{9,10},{10,1... | collective-permute-start | bytes 884744 | tf_op jit(solution)/shard_map/ppermute | solution.py:260
  8.4 15.2 %collective-permute-start.1 = (f32[2,96,384]{2,1,0:T(8,128)}, f32[2,96,384]{2,1,0:T(8,128)S(1)}, u32[]{:S(2)}, u32[]{:S(2)}) collective-permute-start(f32[2,96,384]{2,1,0:T(8,128)} %get-tuple-element.12), channel_id=1, source_target_pairs={{0,7},{1,0},{2,1},{3,2},{4,3},{5,4},{6,5},{7,6},{8,15},{9,8},{10,9... | collective-permute-start | bytes 884744 | tf_op jit(solution)/shard_map/ppermute | solution.py:260
  17.0 1.1 %copy-start = (f32[4,96,384]{2,1,0:T(8,128)S(1)}, f32[4,96,384]{2,1,0:T(8,128)}, u32[]{:S(2)}) copy-start(f32[4,96,384]{2,1,0:T(8,128)} %get-tuple-element.10.keep_ref) | copy-start | bytes 1769476
  18.1 50.1 %copy-start.1 = (f32[1,256,256]{2,1,0:T(8,128)S(1)}, f32[1,256,256]{2,1,0:T(8,128)}, u32[]{:S(2)}) copy-start(f32[1,256,256]{2,1,0:T(8,128)} %prior_ref.1) | copy-start | bytes 786436
  23.6 13.8 %collective-permute-start.2 = (f32[96,384]{1,0:T(8,128)S(1)}, f32[96,384]{1,0:T(8,128)S(1)}, u32[]{:S(2)}, u32[]{:S(2)}) collective-permute-start(f32[96,384]{1,0:T(8,128)S(1)} %shard_map.75.far_ref), channel_id=1, source_target_pairs={{0,4},{1,5},{2,6},{3,7},{4,0},{5,1},{6,2},{7,3},{8,12},{9,13},{10,... | collective-permute-start | bytes 442376 | tf_op jit(solution)/shard_map/ppermute | solution.py:260
  29.1 10.5 %collective-permute-start.3 = (f32[96,384]{1,0:T(8,128)S(1)}, f32[96,384]{1,0:T(8,128)S(1)}, u32[]{:S(2)}, u32[]{:S(2)}) collective-permute-start(f32[96,384]{1,0:T(8,128)S(1)} %get-tuple-element.13), channel_id=1, source_target_pairs={{0,1},{1,2},{2,3},{3,4},{4,5},{5,6},{6,7},{7,0},{8,9},{9,10},{10,1... | collective-permute-start | bytes 442376 | tf_op jit(solution)/shard_map/ppermute | solution.py:260
  32.5 7.4 %collective-permute-start.4 = (f32[96,384]{1,0:T(8,128)S(1)}, f32[96,384]{1,0:T(8,128)S(1)}, u32[]{:S(2)}, u32[]{:S(2)}) collective-permute-start(f32[96,384]{1,0:T(8,128)S(1)} %get-tuple-element.14), channel_id=1, source_target_pairs={{0,7},{1,0},{2,1},{3,2},{4,3},{5,4},{6,5},{7,6},{8,15},{9,8},{10,9... | collective-permute-start | bytes 442376 | tf_op jit(solution)/shard_map/ppermute | solution.py:260
  39.9 3.3 %collective-permute-start.5 = (f32[96,384]{1,0:T(8,128)S(1)}, f32[96,384]{1,0:T(8,128)S(1)}, u32[]{:S(2)}, u32[]{:S(2)}) collective-permute-start(f32[96,384]{1,0:T(8,128)S(1)} %shard_map.78.own_ref), channel_id=1, source_target_pairs={{0,8},{8,0},{1,9},{9,1},{2,10},{10,2},{3,11},{11,3},{4,12},{12,4},... | collective-permute-start | bytes 442376 | tf_op jit(solution)/shard_map/ppermute | solution.py:268

commit v6 on v5

--- a/solution.py
+++ b/solution.py
@@ -43,7 +43,8 @@
     copy_act = pltpu.make_async_copy(act_ref, act, sems.at[1])
     copy_out = pltpu.make_async_copy(out_ref, side_out, sems.at[2])
     copy_len = pltpu.make_async_copy(len_ref, lengths, sems.at[3])
-    parts = [pl.ds(part * half, half) for part in range(2)]
+    spans = [(0, half)] + [(s, s + 1) for s in range(half, seqs)]
+    parts = [pl.ds(start, stop - start) for start, stop in spans]
     copies = [pltpu.make_async_copy(grad_ref.at[p], grad.at[p], grad_sems.at[n]) for n, p in enumerate(parts)]
     copy_len.start()
     copy_in.start()
@@ -61,9 +62,9 @@
         scale = lax.rsqrt(jnp.full(position.shape, lengths[s], jnp.int32).astype(jnp.float32))
         store(s, slice(0, width_in), left * jnp.where(position < lengths[s], scale, 0.0))
     copy_out.wait()
-    for part in range(2):
-        copies[part].wait()
-        for s in range(part * half, (part + 1) * half):
+    for copy, (start, stop) in zip(copies, spans):
+        copy.wait()
+        for s in range(start, stop):
             right = jnp.dot(grad[s], side_out[...], preferred_element_type=jnp.float32)
             store(s, slice(width_in, None), right)
     leave = [
@@ -99,7 +100,7 @@
             pltpu.SMEM(seq_lengths.shape, seq_lengths.dtype),
             pltpu.VMEM((8, rows, width), jnp.float32),
             pltpu.SemaphoreType.DMA((4,)),
-            pltpu.SemaphoreType.DMA((2,)),
+            pltpu.SemaphoreType.DMA((1 + seqs - seqs // 2,)),
             pltpu.SemaphoreType.DMA((3,)),
         ],
         compiler_params=pltpu.CompilerParams(vmem_limit_bytes=PROJECT_VMEM),

time: 69.6 us -> 70.2 us (level)
  no operation moved by 1% of the time
where the time goes in v6:
time: 70.2 us; the launch traced here: 69.9 us
  starting transfers between devices  27.3 us (39%)
  blocking collectives  24 us (34%)
  waiting for transfers between devices  10.6 us (15%)
  Pallas kernels  6.91 us (10%)
  local copies, waits for them, and re-layouts  1.07 us (2%)
    ppermute x5, starting transfers between devices, shift(): lax.ppermute(x, 'tile', [(i, (i + by) % pieces) for i in range(pieces)])  25.3 us
    all_to_all x1, blocking collectives, body(): lax.all_to_all(terms.reshape(owners, 4, width_in), ('tile', 'y'), 0, 0, t...  24 us
    ppermute x5, waiting for transfers between devices, shift(): lax.ppermute(x, 'tile', [(i, (i + by) % pieces) for i in range(pieces)])  9.24 us
    pallas_call x1, Pallas kernels, project(): pl.pallas_call(project_kernel, out_shape=(jax.ShapeDtypeStruct((4, rows,...  4.79 us
    ppermute x1, starting transfers between devices, body(): other = lax.ppermute(own, 'core', [(0, 1), (1, 0)])  1.92 us
  transfers between devices with their start and end apart: 6, of which 6 were waited for; matrix products, arithmetic and copies ran while one was open for 0% of the time, Pallas kernels for 0%

profile of v6, /device:TPU:6, one launch (start us, length us, event | category | flops | bytes accessed | tf_op | source)
XLA Modules:
  0.0 69.9 jit_solution(7008433062159236945)
XLA Ops:
  0.0 4.8 %shard_map.73 = (f32[4,96,384]{2,1,0:T(8,128)}, f32[2,96,384]{2,1,0:T(8,128)}, f32[2,96,384]{2,1,0:T(8,128)}) custom-call(bf16[4,192,512]{2,1,0:T(8,128)(2,1)} %act_ref.1, bf16[4,192,1792]{2,1,0:T(8,128)(2,1)} %grad_ref.1, bf16[512,128]{1,0:T(8,128)(2,1)} %in_ref.1, bf16[1792,256]{1,0:T(8,128)(2,1)} %out_ref.1, s32[4]{0:T(128)} %len_ref.1), custom_call_target="tpu_custom_call" | custom-call | flops 805306368 | bytes 4718592 | tf_op jit(solution)/shard_map/pallas_call | solution.py:86
  4.8 0.0 copy-start.2
  4.8 4.3 %collective-permute-start = (f32[2,96,384]{2,1,0:T(8,128)}, f32[2,96,384]{2,1,0:T(8,128)S(1)}, u32[]{:S(2)}, u32[]{:S(2)}) collective-permute-start(f32[2,96,384]{2,1,0:T(8,128)} %get-tuple-element.11), channel_id=1, source_target_pairs={{0,1},{1,2},{2,3},{3,4},{4,5},{5,6},{6,7},{7,0},{8,9},{9,10},{10,1... | collective-permute-start | bytes 884744 | tf_op jit(solution)/shard_map/ppermute | solution.py:261
  9.1 8.6 %collective-permute-start.1 = (f32[2,96,384]{2,1,0:T(8,128)}, f32[2,96,384]{2,1,0:T(8,128)S(1)}, u32[]{:S(2)}, u32[]{:S(2)}) collective-permute-start(f32[2,96,384]{2,1,0:T(8,128)} %get-tuple-element.12), channel_id=1, source_target_pairs={{0,7},{1,0},{2,1},{3,2},{4,3},{5,4},{6,5},{7,6},{8,15},{9,8},{10,9... | collective-permute-start | bytes 884744 | tf_op jit(solution)/shard_map/ppermute | solution.py:261
  17.7 0.0 copy-start
  17.7 1.1 %copy-done = f32[4,96,384]{2,1,0:T(8,128)S(1)} copy-done((f32[4,96,384]{2,1,0:T(8,128)S(1)}, f32[4,96,384]{2,1,0:T(8,128)}, u32[]{:S(2)}) %copy-start) | copy-done | bytes 589848
  18.8 0.0 copy-start.1
  18.8 4.2 %collective-permute-done.below_ref = f32[2,96,384]{2,1,0:T(8,128)S(1)} collective-permute-done((f32[2,96,384]{2,1,0:T(8,128)}, f32[2,96,384]{2,1,0:T(8,128)S(1)}, u32[]{:S(2)}, u32[]{:S(2)}) %collective-permute-start) | collective-permute-done | bytes 294944 | tf_op jit(solution)/shard_map/ppermute | solution.py:261
  23.0 1.3 %collective-permute-done.1.above_ref = f32[2,96,384]{2,1,0:T(8,128)S(1)} collective-permute-done((f32[2,96,384]{2,1,0:T(8,128)}, f32[2,96,384]{2,1,0:T(8,128)S(1)}, u32[]{:S(2)}, u32[]{:S(2)}) %collective-permute-start.1) | collective-permute-done | bytes 294944 | tf_op jit(solution)/shard_map/ppermute | solution.py:261
  24.3 5.4 %collective-permute-start.2 = (f32[96,384]{1,0:T(8,128)S(1)}, f32[96,384]{1,0:T(8,128)S(1)}, u32[]{:S(2)}, u32[]{:S(2)}) collective-permute-start(f32[96,384]{1,0:T(8,128)S(1)} %shard_map.75.far_ref), channel_id=1, source_target_pairs={{0,4},{1,5},{2,6},{3,7},{4,0},{5,1},{6,2},{7,3},{8,12},{9,13},{10,... | collective-permute-start | bytes 442376 | tf_op jit(solution)/shard_map/ppermute | solution.py:261
  29.8 3.4 %collective-permute-start.3 = (f32[96,384]{1,0:T(8,128)S(1)}, f32[96,384]{1,0:T(8,128)S(1)}, u32[]{:S(2)}, u32[]{:S(2)}) collective-permute-start(f32[96,384]{1,0:T(8,128)S(1)} %get-tuple-element.13), channel_id=1, source_target_pairs={{0,1},{1,2},{2,3},{3,4},{4,5},{5,6},{6,7},{7,0},{8,9},{9,10},{10,1... | collective-permute-start | bytes 442376 | tf_op jit(solution)/shard_map/ppermute | solution.py:261
  33.1 3.7 %collective-permute-start.4 = (f32[96,384]{1,0:T(8,128)S(1)}, f32[96,384]{1,0:T(8,128)S(1)}, u32[]{:S(2)}, u32[]{:S(2)}) collective-permute-start(f32[96,384]{1,0:T(8,128)S(1)} %get-tuple-element.14), channel_id=1, source_target_pairs={{0,7},{1,0},{2,1},{3,2},{4,3},{5,4},{6,5},{7,6},{8,15},{9,8},{10,9... | collective-permute-start | bytes 442376 | tf_op jit(solution)/shard_map/ppermute | solution.py:261
  36.8 1.3 %collective-permute-done.2.far_ref = f32[96,384]{1,0:T(8,128)S(1)} collective-permute-done((f32[96,384]{1,0:T(8,128)S(1)}, f32[96,384]{1,0:T(8,128)S(1)}, u32[]{:S(2)}, u32[]{:S(2)}) %collective-permute-start.2) | collective-permute-done | bytes 147488 | tf_op jit(solution)/shard_map/ppermute | solution.py:261
  38.1 2.1 %collective-permute-done.3.plus_ref = f32[96,384]{1,0:T(8,128)S(1)} collective-permute-done((f32[96,384]{1,0:T(8,128)S(1)}, f32[96,384]{1,0:T(8,128)S(1)}, u32[]{:S(2)}, u32[]{:S(2)}) %collective-permute-start.3) | collective-permute-done | bytes 147488 | tf_op jit(solution)/shard_map/ppermute | solution.py:261
  40.2 0.4 collective-permute-done.4.minus_ref
  40.6 1.9 %collective-permute-start.5 = (f32[96,384]{1,0:T(8,128)S(1)}, f32[96,384]{1,0:T(8,128)S(1)}, u32[]{:S(2)}, u32[]{:S(2)}) collective-permute-start(f32[96,384]{1,0:T(8,128)S(1)} %shard_map.78.own_ref), channel_id=1, source_target_pairs={{0,8},{8,0},{1,9},{9,1},{2,10},{10,2},{3,11},{11,3},{4,12},{12,4},... | collective-permute-start | bytes 442376 | tf_op jit(solution)/shard_map/ppermute | solution.py:269
  42.5 1.3 %collective-permute-done.5.other_ref = f32[96,384]{1,0:T(8,128)S(1)} collective-permute-done((f32[96,384]{1,0:T(8,128)S(1)}, f32[96,384]{1,0:T(8,128)S(1)}, u32[]{:S(2)}, u32[]{:S(2)}) %collective-permute-start.5) | collective-permute-done | bytes 147488 | tf_op jit(solution)/shard_map/ppermute | solution.py:269
  43.9 0.0 copy-done.2
  43.9 1.1 %shard_map.79 = f32[256,128]{1,0:T(8,128)S(1)} custom-call(s32[2,128]{1,0:T(2,128)S(1)} %bitcast.5, f32[96,384]{1,0:T(8,128)S(1)} %shard_map.78.own_ref, f32[96,384]{1,0:T(8,128)S(1)} %collective-permute-done.5.other_ref), custom_call_target="tpu_custom_call" | custom-call | tf_op jit(solution)/shard_map/pallas_call | solution.py:213
  45.0 24.0 %all_to_all.5 = f32[64,4,128]{2,1,0:T(4,128)S(1)} all-to-all(f32[64,4,128]{2,1,0:T(4,128)S(1)} %bitcast.4), channel_id=1, replica_groups=mesh['layer'=4,'y'=8,'core'=2,'tile'=8] {'tile','y'}, dimensions={0} | all-to-all | bytes 262144 | tf_op jit(solution)/shard_map/all_to_all | solution.py:271
  68.9 0.0 copy-done.1
  68.9 0.9 %shard_map.80 = f32[1,256,256]{2,1,0:T(8,128)} custom-call(f32[4,8,8,128]{3,2,1,0:T(8,128)S(1)} %bitcast.3, f32[1,256,256]{2,1,0:T(8,128)S(1)} %copy-done.1), custom_call_target="tpu_custom_call" | custom-call | tf_op jit(solution)/shard_map/pallas_call | solution.py:243
  (5 shorter events, 0.1 us)
Async XLA Ops:
  4.8 39.1 %copy-start.2 = (s32[128,2]{0,1:T(2,128)S(1)}, s32[128,2]{0,1:T(2,128)}, u32[]{:S(2)}) copy-start(s32[128,2]{0,1:T(2,128)} %param.12) | copy-start | bytes 3076
  4.8 18.2 %collective-permute-start = (f32[2,96,384]{2,1,0:T(8,128)}, f32[2,96,384]{2,1,0:T(8,128)S(1)}, u32[]{:S(2)}, u32[]{:S(2)}) collective-permute-start(f32[2,96,384]{2,1,0:T(8,128)} %get-tuple-element.11), channel_id=1, source_target_pairs={{0,1},{1,2},{2,3},{3,4},{4,5},{5,6},{6,7},{7,0},{8,9},{9,10},{10,1... | collective-permute-start | bytes 884744 | tf_op jit(solution)/shard_map/ppermute | solution.py:261
  9.1 15.2 %collective-permute-start.1 = (f32[2,96,384]{2,1,0:T(8,128)}, f32[2,96,384]{2,1,0:T(8,128)S(1)}, u32[]{:S(2)}, u32[]{:S(2)}) collective-permute-start(f32[2,96,384]{2,1,0:T(8,128)} %get-tuple-element.12), channel_id=1, source_target_pairs={{0,7},{1,0},{2,1},{3,2},{4,3},{5,4},{6,5},{7,6},{8,15},{9,8},{10,9... | collective-permute-start | bytes 884744 | tf_op jit(solution)/shard_map/ppermute | solution.py:261
  17.7 1.1 %copy-start = (f32[4,96,384]{2,1,0:T(8,128)S(1)}, f32[4,96,384]{2,1,0:T(8,128)}, u32[]{:S(2)}) copy-start(f32[4,96,384]{2,1,0:T(8,128)} %get-tuple-element.10.keep_ref) | copy-start | bytes 1769476
  18.8 50.2 %copy-start.1 = (f32[1,256,256]{2,1,0:T(8,128)S(1)}, f32[1,256,256]{2,1,0:T(8,128)}, u32[]{:S(2)}) copy-start(f32[1,256,256]{2,1,0:T(8,128)} %prior_ref.1) | copy-start | bytes 786436
  24.3 13.8 %collective-permute-start.2 = (f32[96,384]{1,0:T(8,128)S(1)}, f32[96,384]{1,0:T(8,128)S(1)}, u32[]{:S(2)}, u32[]{:S(2)}) collective-permute-start(f32[96,384]{1,0:T(8,128)S(1)} %shard_map.75.far_ref), channel_id=1, source_target_pairs={{0,4},{1,5},{2,6},{3,7},{4,0},{5,1},{6,2},{7,3},{8,12},{9,13},{10,... | collective-permute-start | bytes 442376 | tf_op jit(solution)/shard_map/ppermute | solution.py:261
  29.8 10.4 %collective-permute-start.3 = (f32[96,384]{1,0:T(8,128)S(1)}, f32[96,384]{1,0:T(8,128)S(1)}, u32[]{:S(2)}, u32[]{:S(2)}) collective-permute-start(f32[96,384]{1,0:T(8,128)S(1)} %get-tuple-element.13), channel_id=1, source_target_pairs={{0,1},{1,2},{2,3},{3,4},{4,5},{5,6},{6,7},{7,0},{8,9},{9,10},{10,1... | collective-permute-start | bytes 442376 | tf_op jit(solution)/shard_map/ppermute | solution.py:261
  33.1 7.4 %collective-permute-start.4 = (f32[96,384]{1,0:T(8,128)S(1)}, f32[96,384]{1,0:T(8,128)S(1)}, u32[]{:S(2)}, u32[]{:S(2)}) collective-permute-start(f32[96,384]{1,0:T(8,128)S(1)} %get-tuple-element.14), channel_id=1, source_target_pairs={{0,7},{1,0},{2,1},{3,2},{4,3},{5,4},{6,5},{7,6},{8,15},{9,8},{10,9... | collective-permute-start | bytes 442376 | tf_op jit(solution)/shard_map/ppermute | solution.py:261
  40.6 3.3 %collective-permute-start.5 = (f32[96,384]{1,0:T(8,128)S(1)}, f32[96,384]{1,0:T(8,128)S(1)}, u32[]{:S(2)}, u32[]{:S(2)}) collective-permute-start(f32[96,384]{1,0:T(8,128)S(1)} %shard_map.78.own_ref), channel_id=1, source_target_pairs={{0,8},{8,0},{1,9},{9,1},{2,10},{10,2},{3,11},{11,3},{4,12},{12,4},... | collective-permute-start | bytes 442376 | tf_op jit(solution)/shard_map/ppermute | solution.py:269
